TPU v7x, 32 devices: a whole 2x2x4 slice. The times are simulated.
32 devices in a mesh: groups: 2 (over x), seq: 16 (over z, y, core).
Axes of the slice: x: 2, y: 2, z: 4, core: 2. Of those that a mesh axis runs over, the one named last changes fastest.
Arguments:
- moe_input: bfloat16 [4096, 1536], P(('groups', 'seq')), parts along dimension 0, may hold values from -6 to 6
- residual_in: bfloat16 [4096, 1536], P(('groups', 'seq')), parts along dimension 0, may hold values from -3 to 3
- expert_ids: int32 [4096, 4], P(('groups', 'seq')), parts along dimension 0, may hold values from 0 to 15, all different within a row; in each aligned block of 128 rows (0 to 127, 128 to 255, ...) at most 64 rows name the same one
- route_logits: float32 [4096, 4], P(('groups', 'seq')), parts along dimension 0, may hold values from -5 to 5
- kept_blocks: int32 [16, 6], P('seq'), may hold values from 0 to 11, as said below
- w_gate: bfloat16 [16, 1536, 768], P('seq'), may hold values from -0.15625 to 0.15625
- w_up: bfloat16 [16, 1536, 768], P('seq'), may hold values from -0.15625 to 0.15625
- w_down: bfloat16 [16, 768, 1536], P('seq'), may hold values from -0.21875 to 0.21875
- norm_gain: float32 [1536], replicated, may hold values from 0.1 to 1.9
- qkv_weight: bfloat16 [1536, 2560], P('seq'), may hold values from -6 to 6
Outputs:
- attention: bfloat16 [4096, 2048], P(('groups', 'seq')), parts along dimension 0
- neuron_energy: float32 [16, 3072], P('seq', 'groups'), parts along dimension 1
There are 2 independent parts, one for each index of `groups`. A program takes and returns all parts, laid end to end along the dimension named above; an argument that names none is the same for every part. Nothing has to cross between parts.
Inputs may be any that keep to these rules, and one draw needn't show every extreme that they name: `expert_ids`: the 4 experts of a token differ; among the 128 tokens of one device no expert is named more than 64 times, a bound that some block reaches. `kept_blocks`: each row names 6 different blocks in increasing order.
All inputs are finite; a program needn't handle non-finite values.
Results may differ from a plain program's by a relative error of at most 0.0095.
Values may be sent and summed in bfloat16 or wider, within the bound.
A program may use at most 128 MiB of HBM per device.

v0:
```python
import jax
import jax.numpy as jnp
from jax import lax
from jax.sharding import PartitionSpec as P

TOP = 4
BLOCK = 128
KB = 6
OB = 12
QH = 32
KVH = 4
HD = 64


def shifted(value, axis, by):
    devices = lax.axis_size(axis)
    return lax.ppermute(value, axis, [(i, (i + by) % devices) for i in range(devices)])


def expert_rows(token_rows, gate_w, up_w, down_w):
    gate_part = jnp.dot(token_rows, gate_w, preferred_element_type=jnp.float32)
    up_part = jnp.dot(token_rows, up_w, preferred_element_type=jnp.float32)
    hidden = jax.nn.silu(gate_part) * up_part
    result = jnp.dot(
        hidden.astype(jnp.bfloat16), down_w, preferred_element_type=jnp.float32
    ).astype(jnp.bfloat16)
    return (result, hidden * hidden)


def attend(running, queries, query_pos, block_rows, key_pos):
    row_max, denom_sum, weighted = running
    key_count = block_rows.shape[0]
    head_width = KVH * HD
    key_part = block_rows[:, :head_width].reshape(key_count, KVH, HD)
    value_part = block_rows[:, head_width:].reshape(key_count, KVH, HD)
    scores = jnp.einsum(
        "tkgd,skd->kgts", queries, key_part, preferred_element_type=jnp.float32
    ) * HD ** (-0.5)
    visible = key_pos[None, :] <= query_pos[:, None]
    scores = jnp.where(visible, scores, -1e30)
    new_max = jnp.maximum(row_max, jnp.max(scores, axis=-1))
    softmax_p = jnp.where(visible, jnp.exp(scores - new_max[..., None]), 0.0)
    factor = jnp.exp(row_max - new_max)
    denom_sum = denom_sum * factor + jnp.sum(softmax_p, axis=-1)
    weighted = weighted * factor[..., None] + jnp.einsum(
        "kgts,skd->kgtd",
        softmax_p.astype(jnp.bfloat16),
        value_part,
        preferred_element_type=jnp.float32,
    )
    return (new_max, denom_sum, weighted)


def attend_quarters(states, queries, query_pos, block_rows, key_pos):
    half_rows = queries.shape[0] // 2
    key_rows = block_rows.shape[0]
    key_halves = 2
    key_step = key_rows // key_halves
    updated = []
    for query_half in range(2):
        current = states[query_half]
        query_part = queries[query_half * half_rows : (query_half + 1) * half_rows]
        qpos_part = query_pos[query_half * half_rows : (query_half + 1) * half_rows]
        for key_half in range(key_halves):
            rows_part = block_rows[key_half * key_step : (key_half + 1) * key_step]
            kpos_part = key_pos[key_half * key_step : (key_half + 1) * key_step]
            current = lax.cond(
                jnp.min(kpos_part) <= jnp.max(qpos_part),
                lambda value, q=query_part, qp=qpos_part, r=rows_part, kp=kpos_part: attend(
                    value, q, qp, r, kp
                ),
                lambda value: value,
                current,
            )
        updated.append(current)
    return tuple(updated)


def on_device(
    moe_input,
    residual_in,
    expert_ids,
    route_logits,
    kept_blocks,
    w_gate,
    w_up,
    w_down,
    norm_gain,
    qkv_weight,
):
    tokens, feat_width = moe_input.shape
    experts = lax.axis_size("seq")
    half_rows = tokens // 2
    slot_cap = min(tokens, max(2, tokens * TOP * 2 // experts))
    flat_ids = expert_ids.reshape(-1)
    onehot = (flat_ids[:, None] == jnp.arange(experts, dtype=jnp.int32)[None, :]).astype(jnp.int32)
    before = jnp.cumsum(onehot, axis=0) - onehot
    slot_index = jnp.sum(before * onehot, axis=1)
    token_rows = jnp.repeat(moe_input, TOP, axis=0)
    outgoing = (
        jnp.zeros((experts, slot_cap, feat_width), jnp.bfloat16)
        .at[flat_ids, slot_index]
        .set(token_rows)
    )
    arrived = lax.all_to_all(outgoing, "seq", split_axis=0, concat_axis=0, tiled=True)
    sources, items, _ = arrived.shape
    result, squares = expert_rows(
        arrived.reshape(sources * items, feat_width), w_gate[0], w_up[0], w_down[0]
    )
    processed, squares = (
        result.reshape(sources, items, feat_width),
        squares.reshape(sources, items, -1),
    )
    energy = jnp.sqrt(jnp.sum(squares, axis=(0, 1)) / (experts * slot_cap) + 1e-06)
    chosen = (kept_blocks[0][:, None] == jnp.arange(OB, dtype=jnp.int32)[None, :]).astype(
        jnp.float32
    )
    placed = jnp.einsum(
        "bo,bc->oc", chosen, energy.reshape(KB, BLOCK), precision=lax.Precision.HIGHEST
    )
    neuron_energy = placed.reshape(1, OB * BLOCK)
    returned = lax.all_to_all(processed, "seq", split_axis=0, concat_axis=0, tiled=True)
    picked = returned[flat_ids, slot_index].astype(jnp.float32).reshape(tokens, TOP, feat_width)
    raised = jnp.exp(route_logits)
    route_weights = raised / jnp.sum(raised, axis=-1, keepdims=True)
    mixed = residual_in.astype(jnp.float32) + jnp.sum(picked * route_weights[..., None], axis=1)
    normed = (
        mixed * lax.rsqrt(jnp.mean(mixed * mixed, axis=-1, keepdims=True) + 1e-05) * norm_gain
    ).astype(jnp.bfloat16)
    my_index = lax.axis_index("seq")
    local_offsets = jnp.arange(tokens, dtype=jnp.int32)

    def place_rows(owner, offsets):
        return owner * tokens + offsets

    projected = jnp.dot(
        normed,
        lax.all_gather(qkv_weight, "seq", axis=0, tiled=True),
        preferred_element_type=jnp.float32,
    ).astype(jnp.bfloat16)
    query_width = QH * HD
    queries = projected[:, :query_width].reshape(tokens, KVH, QH // KVH, HD)
    keys_vals = projected[:, query_width:]
    query_pos = place_rows(my_index, local_offsets)

    def fresh():
        return (
            jnp.full((KVH, QH // KVH, half_rows), -1e30, jnp.float32),
            jnp.zeros((KVH, QH // KVH, half_rows), jnp.float32),
            jnp.zeros((KVH, QH // KVH, half_rows, HD), jnp.float32),
        )

    initial = (fresh(), fresh())
    running = attend_quarters(initial, queries, query_pos, keys_vals, query_pos)

    def cycle_step(shift_step, carried):
        current, block_rows = carried
        block_rows = shifted(block_rows, "seq", -1)
        source = (my_index + shift_step) % experts
        key_pos = place_rows(source, local_offsets)
        current = attend_quarters(current, queries, query_pos, block_rows, key_pos)
        return (current, block_rows)

    running, _ = lax.fori_loop(1, experts, cycle_step, (running, keys_vals))
    pieces = []
    for state in running:
        row_max, denom_sum, weighted = state
        output = weighted / denom_sum[..., None]
        pieces.append(
            output.transpose(2, 0, 1, 3).reshape(half_rows, query_width).astype(jnp.bfloat16)
        )
    attention = jnp.concatenate(pieces, axis=0)
    return (attention, neuron_energy)


def solution(mesh):
    return jax.shard_map(
        on_device,
        mesh=mesh,
        in_specs=(
            P(("groups", "seq"), None),
            P(("groups", "seq"), None),
            P(("groups", "seq"), None),
            P(("groups", "seq"), None),
            P("seq", None),
            P("seq", None, None),
            P("seq", None, None),
            P("seq", None, None),
            P(),
            P("seq", None),
        ),
        out_specs=(P(("groups", "seq"), None), P("seq", "groups")),
        check_vma=False,
    )
```

profile of v0, /device:TPU:29, one launch (start us, length us, event | category | flops | bytes accessed | tf_op | source)
XLA Modules:
  0.0 1170.2 jit_solution(9565457774889533662)
XLA Ops:
  18.3 81.6 %scatter_fusion = bf16[16,64,1536]{2,1,0:T(8,128)(2,1)} fusion(bf16[16,64,1536]{2,1,0:T(8,128)(2,1)} %broadcast_in_dim.132, s32[512]{0:T(512)S(1)} %bitcast.113, bf16[512,1536]{1,0:T(8,128)(2,1)} %reshape.218), kind=kCustom, calls=%fused_computation.1 | custom fusion | bytes 4722688 | tf_op jit(solution)/shard_map/scatter | solution.py:103
  107.1 115.7 %all-to-all-done = bf16[16,64,1536]{2,1,0:T(8,128)(2,1)} async-done(((bf16[16,64,1536]{2,1,0:T(8,128)(2,1)}), bf16[16,64,1536]{2,1,0:T(8,128)(2,1)}, u32[]{:S(2)}, u32[]{:S(2)}) %all-to-all-start) | async-done | bytes 3145760 | tf_op jit(solution)/shard_map/all_to_all | solution.py:105
  251.2 61.1 %all-to-all-done.1 = bf16[16,64,1536]{2,1,0:T(8,128)(2,1)} async-done(((bf16[16,64,1536]{2,1,0:T(8,128)(2,1)}), bf16[16,64,1536]{2,1,0:T(8,128)(2,1)}, u32[]{:S(2)}, u32[]{:S(2)}) %all-to-all-start.1) | async-done | bytes 3145760 | tf_op jit(solution)/shard_map/all_to_all | solution.py:122
  312.3 11.9 %gather_fusion = bf16[512,1536]{1,0:T(8,128)(2,1)} fusion(bf16[16,64,1536]{2,1,0:T(8,128)(2,1)} %all-to-all-done.1, s32[512]{0:T(512)S(1)} %bitcast.112), kind=kCustom, calls=%fused_computation | custom fusion | bytes 3149824 | tf_op jit(solution)/shard_map/gather | solution.py:123
  371.9 785.3 %while.28 = (s32[]{:T(128)}, f32[4,8,64]{2,1,0:T(8,128)}, f32[4,8,64]{2,1,0:T(8,128)}, f32[4,8,64,64]{3,2,1,0:T(8,128)}, f32[4,8,64]{2,1,0:T(8,128)}, /*index=5*...) while((s32[]{:T(128)}, f32[4,8,64]{2,1,0:T(8,128)}, ...), condition=%wide.region_46.47_spmd.clone, body=%wide.region_27.46_spmd.clone.sunk | while | flops 140017936 | bytes 16110998 | solution.py:164
  382.0 11.8 %conditional.22 = ((f32[4,8,64]{2,1,0:T(8,128)}, f32[4,8,64]{2,1,0:T(8,128)}, f32[4,8,64,64]{3,2,1,0:T(8,128)})) conditional(s32[]{:T(128)} %convert_element_type.191, (f32[4,8,64]{2,1,0:T(8,128)}, f32[4,8,64]{2,1,0:T(8,128)}, f32[4,8,64,64]{3,2,1,0:T(8,128)}) %tuple.177, (s32[64]{0:T(128)}, s32[64]{0:T(128)}, bf16[64,512]{1,0:T(8,128)(2,1)S(1)}, ...), branch_computations={%region_38.38_spmd, %region_39.41_spmd} | conditional | flops 35004416 | bytes 3375676 | solution.py:67
  393.7 11.7 %conditional.23 = ((f32[4,8,64]{2,1,0:T(8,128)}, f32[4,8,64]{2,1,0:T(8,128)}, f32[4,8,64,64]{3,2,1,0:T(8,128)})) conditional(s32[]{:T(128)} %convert_element_type.190, (f32[4,8,64]{2,1,0:T(8,128)}, f32[4,8,64]{2,1,0:T(8,128)}, f32[4,8,64,64]{3,2,1,0:T(8,128)}) %get-tuple-element.994, (s32[64]{0:T(128)}, s32[64]{0:T(128)}, ...), branch_computations={%region_42.42_spmd, %region_43.45_spmd} | conditional | flops 35004416 | bytes 3375676 | solution.py:67
  434.3 11.8 %conditional.22 = ((f32[4,8,64]{2,1,0:T(8,128)}, f32[4,8,64]{2,1,0:T(8,128)}, f32[4,8,64,64]{3,2,1,0:T(8,128)})) conditional(s32[]{:T(128)} %convert_element_type.191, (f32[4,8,64]{2,1,0:T(8,128)}, f32[4,8,64]{2,1,0:T(8,128)}, f32[4,8,64,64]{3,2,1,0:T(8,128)}) %tuple.177, (s32[64]{0:T(128)}, s32[64]{0:T(128)}, bf16[64,512]{1,0:T(8,128)(2,1)S(1)}, ...), branch_computations={%region_38.38_spmd, %region_39.41_spmd} | conditional | flops 35004416 | bytes 3375676 | solution.py:67
  446.1 11.7 %conditional.23 = ((f32[4,8,64]{2,1,0:T(8,128)}, f32[4,8,64]{2,1,0:T(8,128)}, f32[4,8,64,64]{3,2,1,0:T(8,128)})) conditional(s32[]{:T(128)} %convert_element_type.190, (f32[4,8,64]{2,1,0:T(8,128)}, f32[4,8,64]{2,1,0:T(8,128)}, f32[4,8,64,64]{3,2,1,0:T(8,128)}) %get-tuple-element.994, (s32[64]{0:T(128)}, s32[64]{0:T(128)}, ...), branch_computations={%region_42.42_spmd, %region_43.45_spmd} | conditional | flops 35004416 | bytes 3375676 | solution.py:67
  486.6 11.8 %conditional.22 = ((f32[4,8,64]{2,1,0:T(8,128)}, f32[4,8,64]{2,1,0:T(8,128)}, f32[4,8,64,64]{3,2,1,0:T(8,128)})) conditional(s32[]{:T(128)} %convert_element_type.191, (f32[4,8,64]{2,1,0:T(8,128)}, f32[4,8,64]{2,1,0:T(8,128)}, f32[4,8,64,64]{3,2,1,0:T(8,128)}) %tuple.177, (s32[64]{0:T(128)}, s32[64]{0:T(128)}, bf16[64,512]{1,0:T(8,128)(2,1)S(1)}, ...), branch_computations={%region_38.38_spmd, %region_39.41_spmd} | conditional | flops 35004416 | bytes 3375676 | solution.py:67
  498.4 11.7 %conditional.23 = ((f32[4,8,64]{2,1,0:T(8,128)}, f32[4,8,64]{2,1,0:T(8,128)}, f32[4,8,64,64]{3,2,1,0:T(8,128)})) conditional(s32[]{:T(128)} %convert_element_type.190, (f32[4,8,64]{2,1,0:T(8,128)}, f32[4,8,64]{2,1,0:T(8,128)}, f32[4,8,64,64]{3,2,1,0:T(8,128)}) %get-tuple-element.994, (s32[64]{0:T(128)}, s32[64]{0:T(128)}, ...), branch_computations={%region_42.42_spmd, %region_43.45_spmd} | conditional | flops 35004416 | bytes 3375676 | solution.py:67
  539.0 11.8 %conditional.22 = ((f32[4,8,64]{2,1,0:T(8,128)}, f32[4,8,64]{2,1,0:T(8,128)}, f32[4,8,64,64]{3,2,1,0:T(8,128)})) conditional(s32[]{:T(128)} %convert_element_type.191, (f32[4,8,64]{2,1,0:T(8,128)}, f32[4,8,64]{2,1,0:T(8,128)}, f32[4,8,64,64]{3,2,1,0:T(8,128)}) %tuple.177, (s32[64]{0:T(128)}, s32[64]{0:T(128)}, bf16[64,512]{1,0:T(8,128)(2,1)S(1)}, ...), branch_computations={%region_38.38_spmd, %region_39.41_spmd} | conditional | flops 35004416 | bytes 3375676 | solution.py:67
  550.7 11.7 %conditional.23 = ((f32[4,8,64]{2,1,0:T(8,128)}, f32[4,8,64]{2,1,0:T(8,128)}, f32[4,8,64,64]{3,2,1,0:T(8,128)})) conditional(s32[]{:T(128)} %convert_element_type.190, (f32[4,8,64]{2,1,0:T(8,128)}, f32[4,8,64]{2,1,0:T(8,128)}, f32[4,8,64,64]{3,2,1,0:T(8,128)}) %get-tuple-element.994, (s32[64]{0:T(128)}, s32[64]{0:T(128)}, ...), branch_computations={%region_42.42_spmd, %region_43.45_spmd} | conditional | flops 35004416 | bytes 3375676 | solution.py:67
  591.3 11.8 %conditional.22 = ((f32[4,8,64]{2,1,0:T(8,128)}, f32[4,8,64]{2,1,0:T(8,128)}, f32[4,8,64,64]{3,2,1,0:T(8,128)})) conditional(s32[]{:T(128)} %convert_element_type.191, (f32[4,8,64]{2,1,0:T(8,128)}, f32[4,8,64]{2,1,0:T(8,128)}, f32[4,8,64,64]{3,2,1,0:T(8,128)}) %tuple.177, (s32[64]{0:T(128)}, s32[64]{0:T(128)}, bf16[64,512]{1,0:T(8,128)(2,1)S(1)}, ...), branch_computations={%region_38.38_spmd, %region_39.41_spmd} | conditional | flops 35004416 | bytes 3375676 | solution.py:67
  603.1 11.7 %conditional.23 = ((f32[4,8,64]{2,1,0:T(8,128)}, f32[4,8,64]{2,1,0:T(8,128)}, f32[4,8,64,64]{3,2,1,0:T(8,128)})) conditional(s32[]{:T(128)} %convert_element_type.190, (f32[4,8,64]{2,1,0:T(8,128)}, f32[4,8,64]{2,1,0:T(8,128)}, f32[4,8,64,64]{3,2,1,0:T(8,128)}) %get-tuple-element.994, (s32[64]{0:T(128)}, s32[64]{0:T(128)}, ...), branch_computations={%region_42.42_spmd, %region_43.45_spmd} | conditional | flops 35004416 | bytes 3375676 | solution.py:67
  643.7 11.8 %conditional.22 = ((f32[4,8,64]{2,1,0:T(8,128)}, f32[4,8,64]{2,1,0:T(8,128)}, f32[4,8,64,64]{3,2,1,0:T(8,128)})) conditional(s32[]{:T(128)} %convert_element_type.191, (f32[4,8,64]{2,1,0:T(8,128)}, f32[4,8,64]{2,1,0:T(8,128)}, f32[4,8,64,64]{3,2,1,0:T(8,128)}) %tuple.177, (s32[64]{0:T(128)}, s32[64]{0:T(128)}, bf16[64,512]{1,0:T(8,128)(2,1)S(1)}, ...), branch_computations={%region_38.38_spmd, %region_39.41_spmd} | conditional | flops 35004416 | bytes 3375676 | solution.py:67
  655.4 11.7 %conditional.23 = ((f32[4,8,64]{2,1,0:T(8,128)}, f32[4,8,64]{2,1,0:T(8,128)}, f32[4,8,64,64]{3,2,1,0:T(8,128)})) conditional(s32[]{:T(128)} %convert_element_type.190, (f32[4,8,64]{2,1,0:T(8,128)}, f32[4,8,64]{2,1,0:T(8,128)}, f32[4,8,64,64]{3,2,1,0:T(8,128)}) %get-tuple-element.994, (s32[64]{0:T(128)}, s32[64]{0:T(128)}, ...), branch_computations={%region_42.42_spmd, %region_43.45_spmd} | conditional | flops 35004416 | bytes 3375676 | solution.py:67
  696.0 11.8 %conditional.22 = ((f32[4,8,64]{2,1,0:T(8,128)}, f32[4,8,64]{2,1,0:T(8,128)}, f32[4,8,64,64]{3,2,1,0:T(8,128)})) conditional(s32[]{:T(128)} %convert_element_type.191, (f32[4,8,64]{2,1,0:T(8,128)}, f32[4,8,64]{2,1,0:T(8,128)}, f32[4,8,64,64]{3,2,1,0:T(8,128)}) %tuple.177, (s32[64]{0:T(128)}, s32[64]{0:T(128)}, bf16[64,512]{1,0:T(8,128)(2,1)S(1)}, ...), branch_computations={%region_38.38_spmd, %region_39.41_spmd} | conditional | flops 35004416 | bytes 3375676 | solution.py:67
  707.8 11.7 %conditional.23 = ((f32[4,8,64]{2,1,0:T(8,128)}, f32[4,8,64]{2,1,0:T(8,128)}, f32[4,8,64,64]{3,2,1,0:T(8,128)})) conditional(s32[]{:T(128)} %convert_element_type.190, (f32[4,8,64]{2,1,0:T(8,128)}, f32[4,8,64]{2,1,0:T(8,128)}, f32[4,8,64,64]{3,2,1,0:T(8,128)}) %get-tuple-element.994, (s32[64]{0:T(128)}, s32[64]{0:T(128)}, ...), branch_computations={%region_42.42_spmd, %region_43.45_spmd} | conditional | flops 35004416 | bytes 3375676 | solution.py:67
  748.4 11.8 %conditional.22 = ((f32[4,8,64]{2,1,0:T(8,128)}, f32[4,8,64]{2,1,0:T(8,128)}, f32[4,8,64,64]{3,2,1,0:T(8,128)})) conditional(s32[]{:T(128)} %convert_element_type.191, (f32[4,8,64]{2,1,0:T(8,128)}, f32[4,8,64]{2,1,0:T(8,128)}, f32[4,8,64,64]{3,2,1,0:T(8,128)}) %tuple.177, (s32[64]{0:T(128)}, s32[64]{0:T(128)}, bf16[64,512]{1,0:T(8,128)(2,1)S(1)}, ...), branch_computations={%region_38.38_spmd, %region_39.41_spmd} | conditional | flops 35004416 | bytes 3375676 | solution.py:67
  760.1 11.7 %conditional.23 = ((f32[4,8,64]{2,1,0:T(8,128)}, f32[4,8,64]{2,1,0:T(8,128)}, f32[4,8,64,64]{3,2,1,0:T(8,128)})) conditional(s32[]{:T(128)} %convert_element_type.190, (f32[4,8,64]{2,1,0:T(8,128)}, f32[4,8,64]{2,1,0:T(8,128)}, f32[4,8,64,64]{3,2,1,0:T(8,128)}) %get-tuple-element.994, (s32[64]{0:T(128)}, s32[64]{0:T(128)}, ...), branch_computations={%region_42.42_spmd, %region_43.45_spmd} | conditional | flops 35004416 | bytes 3375676 | solution.py:67
  800.7 11.8 %conditional.22 = ((f32[4,8,64]{2,1,0:T(8,128)}, f32[4,8,64]{2,1,0:T(8,128)}, f32[4,8,64,64]{3,2,1,0:T(8,128)})) conditional(s32[]{:T(128)} %convert_element_type.191, (f32[4,8,64]{2,1,0:T(8,128)}, f32[4,8,64]{2,1,0:T(8,128)}, f32[4,8,64,64]{3,2,1,0:T(8,128)}) %tuple.177, (s32[64]{0:T(128)}, s32[64]{0:T(128)}, bf16[64,512]{1,0:T(8,128)(2,1)S(1)}, ...), branch_computations={%region_38.38_spmd, %region_39.41_spmd} | conditional | flops 35004416 | bytes 3375676 | solution.py:67
  812.5 11.7 %conditional.23 = ((f32[4,8,64]{2,1,0:T(8,128)}, f32[4,8,64]{2,1,0:T(8,128)}, f32[4,8,64,64]{3,2,1,0:T(8,128)})) conditional(s32[]{:T(128)} %convert_element_type.190, (f32[4,8,64]{2,1,0:T(8,128)}, f32[4,8,64]{2,1,0:T(8,128)}, f32[4,8,64,64]{3,2,1,0:T(8,128)}) %get-tuple-element.994, (s32[64]{0:T(128)}, s32[64]{0:T(128)}, ...), branch_computations={%region_42.42_spmd, %region_43.45_spmd} | conditional | flops 35004416 | bytes 3375676 | solution.py:67
  853.0 11.8 %conditional.22 = ((f32[4,8,64]{2,1,0:T(8,128)}, f32[4,8,64]{2,1,0:T(8,128)}, f32[4,8,64,64]{3,2,1,0:T(8,128)})) conditional(s32[]{:T(128)} %convert_element_type.191, (f32[4,8,64]{2,1,0:T(8,128)}, f32[4,8,64]{2,1,0:T(8,128)}, f32[4,8,64,64]{3,2,1,0:T(8,128)}) %tuple.177, (s32[64]{0:T(128)}, s32[64]{0:T(128)}, bf16[64,512]{1,0:T(8,128)(2,1)S(1)}, ...), branch_computations={%region_38.38_spmd, %region_39.41_spmd} | conditional | flops 35004416 | bytes 3375676 | solution.py:67
  905.4 11.8 %conditional.22 = ((f32[4,8,64]{2,1,0:T(8,128)}, f32[4,8,64]{2,1,0:T(8,128)}, f32[4,8,64,64]{3,2,1,0:T(8,128)})) conditional(s32[]{:T(128)} %convert_element_type.191, (f32[4,8,64]{2,1,0:T(8,128)}, f32[4,8,64]{2,1,0:T(8,128)}, f32[4,8,64,64]{3,2,1,0:T(8,128)}) %tuple.177, (s32[64]{0:T(128)}, s32[64]{0:T(128)}, bf16[64,512]{1,0:T(8,128)(2,1)S(1)}, ...), branch_computations={%region_38.38_spmd, %region_39.41_spmd} | conditional | flops 35004416 | bytes 3375676 | solution.py:67
  917.1 11.7 %conditional.23 = ((f32[4,8,64]{2,1,0:T(8,128)}, f32[4,8,64]{2,1,0:T(8,128)}, f32[4,8,64,64]{3,2,1,0:T(8,128)})) conditional(s32[]{:T(128)} %convert_element_type.190, (f32[4,8,64]{2,1,0:T(8,128)}, f32[4,8,64]{2,1,0:T(8,128)}, f32[4,8,64,64]{3,2,1,0:T(8,128)}) %get-tuple-element.994, (s32[64]{0:T(128)}, s32[64]{0:T(128)}, ...), branch_computations={%region_42.42_spmd, %region_43.45_spmd} | conditional | flops 35004416 | bytes 3375676 | solution.py:67
  957.7 11.8 %conditional.22 = ((f32[4,8,64]{2,1,0:T(8,128)}, f32[4,8,64]{2,1,0:T(8,128)}, f32[4,8,64,64]{3,2,1,0:T(8,128)})) conditional(s32[]{:T(128)} %convert_element_type.191, (f32[4,8,64]{2,1,0:T(8,128)}, f32[4,8,64]{2,1,0:T(8,128)}, f32[4,8,64,64]{3,2,1,0:T(8,128)}) %tuple.177, (s32[64]{0:T(128)}, s32[64]{0:T(128)}, bf16[64,512]{1,0:T(8,128)(2,1)S(1)}, ...), branch_computations={%region_38.38_spmd, %region_39.41_spmd} | conditional | flops 35004416 | bytes 3375676 | solution.py:67
  969.5 11.7 %conditional.23 = ((f32[4,8,64]{2,1,0:T(8,128)}, f32[4,8,64]{2,1,0:T(8,128)}, f32[4,8,64,64]{3,2,1,0:T(8,128)})) conditional(s32[]{:T(128)} %convert_element_type.190, (f32[4,8,64]{2,1,0:T(8,128)}, f32[4,8,64]{2,1,0:T(8,128)}, f32[4,8,64,64]{3,2,1,0:T(8,128)}) %get-tuple-element.994, (s32[64]{0:T(128)}, s32[64]{0:T(128)}, ...), branch_computations={%region_42.42_spmd, %region_43.45_spmd} | conditional | flops 35004416 | bytes 3375676 | solution.py:67
  1010.1 11.8 %conditional.22 = ((f32[4,8,64]{2,1,0:T(8,128)}, f32[4,8,64]{2,1,0:T(8,128)}, f32[4,8,64,64]{3,2,1,0:T(8,128)})) conditional(s32[]{:T(128)} %convert_element_type.191, (f32[4,8,64]{2,1,0:T(8,128)}, f32[4,8,64]{2,1,0:T(8,128)}, f32[4,8,64,64]{3,2,1,0:T(8,128)}) %tuple.177, (s32[64]{0:T(128)}, s32[64]{0:T(128)}, bf16[64,512]{1,0:T(8,128)(2,1)S(1)}, ...), branch_computations={%region_38.38_spmd, %region_39.41_spmd} | conditional | flops 35004416 | bytes 3375676 | solution.py:67
  1062.4 11.8 %conditional.22 = ((f32[4,8,64]{2,1,0:T(8,128)}, f32[4,8,64]{2,1,0:T(8,128)}, f32[4,8,64,64]{3,2,1,0:T(8,128)})) conditional(s32[]{:T(128)} %convert_element_type.191, (f32[4,8,64]{2,1,0:T(8,128)}, f32[4,8,64]{2,1,0:T(8,128)}, f32[4,8,64,64]{3,2,1,0:T(8,128)}) %tuple.177, (s32[64]{0:T(128)}, s32[64]{0:T(128)}, bf16[64,512]{1,0:T(8,128)(2,1)S(1)}, ...), branch_computations={%region_38.38_spmd, %region_39.41_spmd} | conditional | flops 35004416 | bytes 3375676 | solution.py:67
  1074.2 11.7 %conditional.23 = ((f32[4,8,64]{2,1,0:T(8,128)}, f32[4,8,64]{2,1,0:T(8,128)}, f32[4,8,64,64]{3,2,1,0:T(8,128)})) conditional(s32[]{:T(128)} %convert_element_type.190, (f32[4,8,64]{2,1,0:T(8,128)}, f32[4,8,64]{2,1,0:T(8,128)}, f32[4,8,64,64]{3,2,1,0:T(8,128)}) %get-tuple-element.994, (s32[64]{0:T(128)}, s32[64]{0:T(128)}, ...), branch_computations={%region_42.42_spmd, %region_43.45_spmd} | conditional | flops 35004416 | bytes 3375676 | solution.py:67
  1114.7 11.8 %conditional.22 = ((f32[4,8,64]{2,1,0:T(8,128)}, f32[4,8,64]{2,1,0:T(8,128)}, f32[4,8,64,64]{3,2,1,0:T(8,128)})) conditional(s32[]{:T(128)} %convert_element_type.191, (f32[4,8,64]{2,1,0:T(8,128)}, f32[4,8,64]{2,1,0:T(8,128)}, f32[4,8,64,64]{3,2,1,0:T(8,128)}) %tuple.177, (s32[64]{0:T(128)}, s32[64]{0:T(128)}, bf16[64,512]{1,0:T(8,128)(2,1)S(1)}, ...), branch_computations={%region_38.38_spmd, %region_39.41_spmd} | conditional | flops 35004416 | bytes 3375676 | solution.py:67
  (957 shorter events, 1139.9 us)
Async XLA Ops:
  7.2 226.0 %copy-start = (bf16[1,768,1536]{2,1,0:T(8,128)(2,1)S(1)}, bf16[1,768,1536]{2,1,0:T(8,128)(2,1)}, u32[]{:S(2)}) copy-start(bf16[1,768,1536]{2,1,0:T(8,128)(2,1)} %param.35) | copy-start | bytes 7077892
  99.9 122.9 %all-to-all-start = ((bf16[16,64,1536]{2,1,0:T(8,128)(2,1)}), bf16[16,64,1536]{2,1,0:T(8,128)(2,1)}, u32[]{:S(2)}, u32[]{:S(2)}) async-start(bf16[16,64,1536]{2,1,0:T(8,128)(2,1)} %scatter_fusion), calls=%async_computation | async-start | bytes 6291456 | tf_op jit(solution)/shard_map/all_to_all | solution.py:105
  106.4 226.9 %all-gather.2.cloned.1.call-start = ((), (), s32[]{:S(2)}) async-start(), calls=%async_computation.2 | async-start | bytes 8355840 | tf_op jit(solution)/shard_map/all_gather | solution.py:138
  222.8 5.4 copy-start.12
  237.2 12.3 %copy-start.11 = (f32[128,4]{0,1:T(4,128)S(1)}, f32[128,4]{0,1:T(4,128)}, u32[]{:S(2)}) copy-start(f32[128,4]{0,1:T(4,128)} %param.31) | copy-start | bytes 6148
  237.2 13.1 %copy-start.13 = (s32[1,6]{1,0:T(1,128)S(1)}, s32[1,6]{1,0:T(1,128)}, u32[]{:S(2)}) copy-start(s32[1,6]{1,0:T(1,128)} %param.32) | copy-start | bytes 76
  237.2 75.0 %all-to-all-start.1 = ((bf16[16,64,1536]{2,1,0:T(8,128)(2,1)}), bf16[16,64,1536]{2,1,0:T(8,128)(2,1)}, u32[]{:S(2)}, u32[]{:S(2)}) async-start(bf16[16,64,1536]{2,1,0:T(8,128)(2,1)} %bitcast.122), calls=%async_computation.1 | async-start | bytes 6291456 | tf_op jit(solution)/shard_map/all_to_all | solution.py:122
  328.4 4.9 copy-start.9
  337.9 14.9 %copy-start.7 = (bf16[64,512]{1,0:T(8,128)(2,1)}, bf16[64,512]{1,0:T(8,128)(2,1)S(1)}, u32[]{:S(2)}) copy-start(bf16[64,512]{1,0:T(8,128)(2,1)S(1)} %get-tuple-element.755) | copy-start | bytes 196612
  371.9 9.4 collective-permute-start
  406.2 4.8 copy-start.5
  424.5 9.2 collective-permute-start
  458.5 4.8 copy-start.5
  476.8 9.2 collective-permute-start
  529.2 9.2 collective-permute-start
  563.2 4.8 copy-start.5
  581.5 9.2 collective-permute-start
  615.6 4.8 copy-start.5
  633.8 9.2 collective-permute-start
  686.2 9.2 collective-permute-start
  720.2 4.8 copy-start.5
  738.5 9.2 collective-permute-start
  790.9 9.2 collective-permute-start
  843.2 9.2 collective-permute-start
  877.3 4.8 copy-start.5
  895.6 9.2 collective-permute-start
  929.6 4.8 copy-start.5
  947.9 9.2 collective-permute-start
  982.0 4.8 copy-start.5
  1000.2 9.2 collective-permute-start
  1052.6 9.2 collective-permute-start
  1104.9 9.2 collective-permute-start
  (56 other events, 141.7 us)
Sparse Core Ops, SparseCore 0:
  109.5 110.4 all-gather.1
where the time goes:
time: 1190 us; the launch traced here: 1170 us
  local copies, waits for them, and re-layouts  329 us (28%)
  matrix products  302 us (25%)
  other arithmetic  254 us (21%)
  waiting for transfers between devices  177 us (15%)
  loops' own time  76.1 us (6%)
  between operations  19.2 us (2%)
  starting transfers between devices  12.8 us (1%)
    dot_general x63, matrix products, attend(): jnp.einsum('kgts,skd->kgtd', softmax_p.astype(jnp.bfloat16), value_part,...  176 us
    all_to_all x1, waiting for transfers between devices, on_device(): lax.all_to_all(outgoing, 'seq', split_axis=0, concat_axis=0, tiled=True)  116 us
    dot_general x63, matrix products, attend(): jnp.einsum('tkgd,skd->kgts', queries, key_part, preferred_element_type=jn...  107 us
    add x63, other arithmetic, attend(): denom_sum = denom_sum * factor + jnp.sum(softmax_p, axis=-1)  85.5 us
    scatter x1, local copies, waits for them, and re-layouts, on_device(): outgoing = jnp.zeros((experts, slot_cap, feat_width), jnp.bfloat16).at[fl...  81.6 us
    another operation x1, loops' own time, on_device(): running, _ = lax.fori_loop(1, experts, cycle_step, (running, keys_vals))  73.7 us
    reshape x63, local copies, waits for them, and re-layouts, attend(): value_part = block_rows[:, head_width:].reshape(key_count, KVH, HD)  62.8 us
    all_to_all x1, waiting for transfers between devices, on_device(): lax.all_to_all(processed, 'seq', split_axis=0, concat_axis=0, tiled=True)  61.1 us
  transfers between devices with their start and end apart: 18, of which 2 were waited for; matrix products, arithmetic and copies ran while one was open for 9% of the time, Pallas kernels for 0%

commit v1 on v0

v1 whole, which is shorter than its diff:
```python
import functools

import jax
import jax.numpy as jnp
from jax import lax
from jax.experimental import pallas as pl
from jax.experimental.pallas import tpu as pltpu
from jax.sharding import PartitionSpec as P

TOP = 4
BLOCK = 128
KB = 6
OB = 12
QH = 32
KVH = 4
HD = 64
BK = 256
QCHUNK = 512
F32 = jnp.float32
BF16 = jnp.bfloat16


def attention_kernel(qt_ref, kv_ref, out_ref, q_scr, m_scr, l_scr, acc_scr):
    me = lax.axis_index("seq")
    tokens = qt_ref.shape[1]
    heads = QCHUNK // tokens
    chunks = QH // heads
    for c in range(chunks):
        for h in range(heads):
            row = (c * heads + h) * HD
            q_scr[c, :, h * tokens : (h + 1) * tokens] = qt_ref[row : row + HD, :]
    m_scr[...] = jnp.full_like(m_scr, -1e30)
    l_scr[...] = jnp.zeros_like(l_scr)
    acc_scr[...] = jnp.zeros_like(acc_scr)

    def block(kb, masked):
        start = pl.multiple_of(kb * BK, BK)
        if masked:
            key_pos = start + lax.broadcasted_iota(jnp.int32, (BK, tokens), 0)
            query_pos = me * tokens + lax.broadcasted_iota(jnp.int32, (BK, tokens), 1)
            hide = jnp.where(key_pos <= query_pos, 0.0, -1e30)
            hide = jnp.concatenate([hide] * heads, axis=1)
        for c in range(chunks):
            g = c * heads // (QH // KVH)
            keys = kv_ref[pl.ds(start, BK), g * HD : (g + 1) * HD]
            vals = kv_ref[pl.ds(start, BK), (KVH + g) * HD : (KVH + g + 1) * HD]
            s = jnp.dot(keys, q_scr[c], preferred_element_type=F32)
            if masked:
                s = s + hide
            m_old = m_scr[c]
            m_new = jnp.maximum(m_old, jnp.max(s, axis=0, keepdims=True))
            p = jnp.exp(s - m_new)
            alpha = jnp.exp(m_old - m_new)
            m_scr[c] = m_new
            l_scr[c] = l_scr[c] * alpha + jnp.sum(p, axis=0, keepdims=True)
            pv = lax.dot_general(
                vals, p.astype(BF16), (((0,), (0,)), ((), ())), preferred_element_type=F32
            )
            acc_scr[c] = acc_scr[c] * alpha + pv

    full = me * tokens // BK

    @pl.loop(0, full)
    def _(kb):
        block(kb, False)

    block(full, True)
    for c in range(chunks):
        o = acc_scr[c] / l_scr[c]
        for h in range(0, heads, 2):
            pair = jnp.concatenate(
                [o[:, h * tokens : (h + 1) * tokens], o[:, (h + 1) * tokens : (h + 2) * tokens]], axis=0
            )
            col = (c * heads + h) * HD
            out_ref[:, col : col + 2 * HD] = pair.T.astype(BF16)


def attention_call(qt, kv):
    tokens = qt.shape[1]
    chunks = QH * tokens // QCHUNK
    return pl.pallas_call(
        attention_kernel,
        out_shape=jax.ShapeDtypeStruct((tokens, QH * HD), BF16),
        in_specs=[pl.BlockSpec(memory_space=pltpu.VMEM)] * 2,
        out_specs=pl.BlockSpec(memory_space=pltpu.VMEM),
        scratch_shapes=[
            pltpu.VMEM((chunks, HD, QCHUNK), BF16),
            pltpu.VMEM((chunks, 1, QCHUNK), F32),
            pltpu.VMEM((chunks, 1, QCHUNK), F32),
            pltpu.VMEM((chunks, HD, QCHUNK), F32),
        ],
        compiler_params=pltpu.CompilerParams(vmem_limit_bytes=40 * 1024 * 1024),
        name="attention",
    )(qt, kv)


def on_device(
    moe_input,
    residual_in,
    expert_ids,
    route_logits,
    kept_blocks,
    w_gate,
    w_up,
    w_down,
    norm_gain,
    qkv_weight,
):
    tokens, width = moe_input.shape
    seq = lax.axis_size("seq")
    me = lax.axis_index("seq")
    cap = min(tokens, max(2, tokens * TOP * 2 // seq))
    raised = jnp.exp(route_logits)
    weights = raised / jnp.sum(raised, axis=-1, keepdims=True)
    meta = jnp.concatenate([expert_ids.astype(F32), weights], axis=1)
    meta = lax.all_gather(meta, "seq", axis=0, tiled=True)
    rows = lax.all_gather(moe_input, "seq", axis=0, tiled=True)
    qkv_full = lax.all_gather(qkv_weight, "seq", axis=0, tiled=True)

    hit = (meta[:, :TOP] == me.astype(F32)).astype(F32)
    share = jnp.sum(hit * meta[:, TOP:], axis=1).reshape(seq, tokens)
    named = jnp.sum(hit, axis=1).reshape(seq, tokens)
    earlier = (jnp.arange(tokens)[:, None] < jnp.arange(tokens)[None, :]).astype(F32)
    slot = jnp.dot(named, earlier)
    slot = jnp.where(named > 0.5, slot, -1.0)
    place = (slot[:, None, :] == jnp.arange(cap, dtype=F32)[None, :, None]).astype(BF16)
    sent = jnp.einsum(
        "sct,std->scd", place, rows.reshape(seq, tokens, width), preferred_element_type=F32
    ).astype(BF16).reshape(seq * cap, width)
    gate_part = jnp.dot(sent, w_gate[0], preferred_element_type=F32)
    up_part = jnp.dot(sent, w_up[0], preferred_element_type=F32)
    hidden = jax.nn.silu(gate_part) * up_part
    energy = jnp.sqrt(jnp.sum(hidden * hidden, axis=0) / (seq * cap) + 1e-06)
    result = jnp.dot(hidden.astype(BF16), w_down[0], preferred_element_type=F32).astype(BF16)
    chosen = (kept_blocks[0][:, None] == jnp.arange(OB, dtype=jnp.int32)[None, :]).astype(F32)
    placed = jnp.einsum(
        "bo,bc->oc", chosen, energy.reshape(KB, BLOCK), precision=lax.Precision.HIGHEST
    )
    neuron_energy = placed.reshape(1, OB * BLOCK)
    back = jnp.einsum(
        "sct,scd->std", place, result.reshape(seq, cap, width), preferred_element_type=F32
    )
    partial = (back * share[..., None]).astype(BF16).reshape(seq * tokens, width)
    moe = lax.psum_scatter(partial, "seq", scatter_dimension=0, tiled=True)
    mixed = residual_in.astype(F32) + moe.astype(F32)
    normed = (
        mixed * lax.rsqrt(jnp.mean(mixed * mixed, axis=-1, keepdims=True) + 1e-05) * norm_gain
    ).astype(BF16)
    query_width = QH * HD
    keys_vals = jnp.dot(normed, qkv_full[:, query_width:], preferred_element_type=F32).astype(BF16)
    kv = lax.all_gather(keys_vals, "seq", axis=0, tiled=True)
    queries = jnp.dot(normed, qkv_full[:, :query_width], preferred_element_type=F32).astype(BF16)
    attention = attention_call((queries * HD ** (-0.5)).T, kv)
    return (attention, neuron_energy)


def solution(mesh):
    return jax.shard_map(
        on_device,
        mesh=mesh,
        in_specs=(
            P(("groups", "seq"), None),
            P(("groups", "seq"), None),
            P(("groups", "seq"), None),
            P(("groups", "seq"), None),
            P("seq", None),
            P("seq", None, None),
            P("seq", None, None),
            P("seq", None, None),
            P(),
            P("seq", None),
        ),
        out_specs=(P(("groups", "seq"), None), P("seq", "groups")),
        check_vma=False,
    )
```

time: 1190 us -> 319 us (0.27); the launches traced: 1170 us -> 319 us
  local copies, waits for them, and re-layouts: 329 us -> 2.24 us
  matrix products: 302 us -> 25.5 us
  other arithmetic: 254 us -> 3.35 us
  loops' own time: 76.1 us -> 0 us
  waiting for transfers between devices: 177 us -> 234 us
  Pallas kernels: 0 us -> 22.5 us
  blocking collectives: 0 us -> 17.2 us
  starting transfers between devices: 12.8 us -> 0.34 us
    dot_general x130 -> x8, matrix products: 302 us -> 25.3 us  [the longest x1 5.52 us: on_device(): jnp.dot(normed, qkv_full[:, :query_width], preferred_element_type=F32)]
    all_to_all x2 -> x0, waiting for transfers between devices: 177 us -> none  [the longest x1 116 us: on_device(): lax.all_to_all(outgoing, 'seq', split_axis=0, concat_axis=0, tiled=True)]
    all_gather x1 -> x3, waiting for transfers between devices: 0.01 us -> 150 us  [the longest x1 72.1 us: on_device(): qkv_full = lax.all_gather(qkv_weight, 'seq', axis=0, tiled=True)]
    reshape x128 -> x0, local copies, waits for them, and re-layouts: 92.5 us -> none  [the longest x63 62.8 us: attend(): value_part = block_rows[:, head_width:].reshape(key_count, KVH, HD)]
    add x79 -> x0, other arithmetic: 85.5 us -> none  [the longest x63 85.5 us: attend(): denom_sum = denom_sum * factor + jnp.sum(softmax_p, axis=-1)]
    reduce_scatter x0 -> x1, waiting for transfers between devices: none -> 82.8 us  [on_device(): moe = lax.psum_scatter(partial, 'seq', scatter_dimension=0, tiled=True)]
    scatter x1 -> x0, local copies, waits for them, and re-layouts: 81.6 us -> none  [on_device(): outgoing = jnp.zeros((experts, slot_cap, feat_width), jnp.bfloat16).at[fl...]
    another operation x65 -> x0, loops' own time: 76.1 us -> none  [the longest x1 73.7 us: on_device(): running, _ = lax.fori_loop(1, experts, cycle_step, (running, keys_vals))]
  transfers between devices with their start and end apart: 18 -> 4, of which waited for: 2 -> 4; matrix products, arithmetic and copies ran while one was open for 9% -> 3% of each run, Pallas kernels for 0% -> 0%
where the time goes in v1:
time: 319 us
  waiting for transfers between devices  234 us (73%)
  matrix products  25.5 us (8%)
  Pallas kernels  22.5 us (7%)
  blocking collectives  17.2 us (5%)
  between operations  13.9 us (4%)
  other arithmetic  3.35 us (1%)
    reduce_scatter x1, waiting for transfers between devices, on_device(): moe = lax.psum_scatter(partial, 'seq', scatter_dimension=0, tiled=True)  82.8 us
    all_gather x1, waiting for transfers between devices, on_device(): qkv_full = lax.all_gather(qkv_weight, 'seq', axis=0, tiled=True)  72.1 us
    all_gather x1, waiting for transfers between devices, on_device(): rows = lax.all_gather(moe_input, 'seq', axis=0, tiled=True)  43.9 us
    all_gather x1, waiting for transfers between devices, on_device(): kv = lax.all_gather(keys_vals, 'seq', axis=0, tiled=True)  33.9 us
    pallas_call x1, Pallas kernels, attention_call(): pl.pallas_call(attention_kernel, out_shape=jax.ShapeDtypeStruct((tokens,...  22.5 us
    all_gather x1, blocking collectives, on_device(): meta = lax.all_gather(meta, 'seq', axis=0, tiled=True)  17.2 us
  transfers between devices with their start and end apart: 4, of which 4 were waited for; matrix products, arithmetic and copies ran while one was open for 3% of the time, Pallas kernels for 0%

profile of v1, /device:TPU:29, one launch (start us, length us, event | category | flops | bytes accessed | tf_op | source)
XLA Modules:
  0.0 319.1 jit_solution(13789797422582215315)
XLA Ops:
  7.2 0.0 copy-start
  7.2 0.0 all-gather.4.cloned.1.call-start
  7.2 0.7 all-gather.4.cloned.1.call-update
  7.9 0.0 reduce-scatter.2.cloned.1.call-start
  8.0 0.7 convert_element_type.42
  8.6 0.7 exponential_reduce_fusion
  9.3 0.7 exponential_divide_fusion
  10.1 17.2 %all_gather.12 = f32[2048,8]{0,1:T(8,128)S(1)} all-gather(f32[128,8]{0,1:T(8,128)S(1)} %pad_maximum_fusion), channel_id=1, replica_groups=mesh['groups'=2,'seq'=16] {'seq'}, dimensions={0}, use_global_device_ids=true | all-gather | bytes 69632 | tf_op jit(solution)/shard_map/all_gather | solution.py:116
  27.3 0.1 convolution_select_fusion
  27.5 43.9 %all-gather.4.cloned.1.call-done = bf16[2048,1536]{1,0:T(8,128)(2,1)} async-done(((bf16[128,1536]{1,0:T(8,128)(2,1)}), bf16[2048,1536]{1,0:T(8,128)(2,1)}) %all-gather.4.cloned.1.call-update) | async-done | bytes 6291472 | tf_op jit(solution)/shard_map/all_gather | solution.py:117
  71.4 3.9 %convolution_convert_fusion.1 = bf16[16,64,1536]{2,1,0:T(8,128)(2,1)S(1)} fusion(bf16[16,128,1536]{2,1,0:T(8,128)(2,1)} %bitcast.42, f32[16,128]{1,0:T(8,128)S(1)} %convolution_select_fusion), kind=kOutput, calls=%fused_computation.4 | convolution fusion | flops 404357120 | bytes 9445376 | tf_op jit(solution)/shard_map/sct,std->scd/dot_general | solution.py:127
  75.4 0.0 copy-start.4
  75.4 2.6 fusion.6
  78.0 3.1 multiply_reduce_fusion
  81.1 2.8 convolution_convert_fusion
  83.9 4.6 %multiply_convert_fusion = bf16[16,128,1536]{2,1,0:T(8,128)(2,1)} fusion(bf16[16,64,1536]{2,1,0:T(8,128)(2,1)S(1)} %bitcast.45, f32[16,128]{1,0:T(8,128)S(1)} %bitcast.46, f32[16,128]{1,0:T(8,128)S(1)} %convolution_select_fusion), kind=kOutput, calls=%fused_computation | convolution fusion | flops 409075712 | bytes 9453568 | tf_op jit(solution)/shard_map/sct,scd->std/dot_general | solution.py:140
  88.5 0.0 reduce-scatter.2.cloned.1.call-update
  88.5 0.0 copy-start.6
  88.5 0.0 all-gather.6.cloned.1.call-start
  88.6 0.7 all-gather.6.cloned.1.call-update
  89.3 0.2 all-gather.8.cloned.1.call-start
  89.5 82.8 %reduce-scatter.2.cloned.1.call-done = bf16[128,1536]{1,0:T(8,128)(2,1)} async-done(((bf16[2048,1536]{1,0:T(8,128)(2,1)}), bf16[128,1536]{1,0:T(8,128)(2,1)}) %reduce-scatter.2.cloned.1.call-update) | async-done | bytes 393232 | tf_op jit(solution)/shard_map/reduce_scatter | solution.py:144
  172.3 1.2 multiply_reduce_fusion.1
  173.5 72.1 %all-gather.6.cloned.1.call-done = bf16[1536,2560]{1,0:T(8,128)(2,1)} async-done(((bf16[96,2560]{1,0:T(8,128)(2,1)}), bf16[1536,2560]{1,0:T(8,128)(2,1)}) %all-gather.6.cloned.1.call-update) | async-done | bytes 7864336 | tf_op jit(solution)/shard_map/all_gather | solution.py:118
  245.5 2.6 fusion.21
  248.2 0.0 all-gather.8.cloned.1.call-update
  248.2 0.3 convolution_bitcast_fusion
  248.4 0.6 copy.16
  249.1 5.5 %fusion.13.qt_ref = bf16[2048,128]{1,0:T(8,128)(2,1)S(1)} fusion(bf16[1536,2560]{1,0:T(8,128)(2,1)} %all-gather.6.cloned.1.call-done, bf16[128,1536]{1,0:T(8,128)(2,1)} %reduce-scatter.2.cloned.1.call-done, bf16[128,1536]{1,0:T(8,128)(2,1)S(1)} %copy-done.2, f32[1536]{0:T(1024)S(1)} %copy-done.5, f32[128]{0:T(128)S(1)} %add_rsqrt_fusion), kind=kOutput, calls=%fused_computation.14 | convolution fusion | flops 807010304 | bytes 7608832 | tf_op jit(solution)/shard_map/dot_general | solution.py:152
  254.6 33.9 %all-gather.8.cloned.1.call-done.kv_ref = bf16[2048,512]{1,0:T(8,128)(2,1)} async-done(((bf16[128,512]{1,0:T(8,128)(2,1)}), bf16[2048,512]{1,0:T(8,128)(2,1)}) %all-gather.8.cloned.1.call-update) | async-done | bytes 2097168 | tf_op jit(solution)/shard_map/all_gather | solution.py:151
  288.5 1.6 copy-done.1
  290.1 22.5 %attention.1 = bf16[128,2048]{1,0:T(8,128)(2,1)} custom-call(bf16[2048,128]{1,0:T(8,128)(2,1)S(1)} %fusion.13.qt_ref, bf16[2048,512]{1,0:T(8,128)(2,1)S(1)} %copy-done.1), custom_call_target="tpu_custom_call" | custom-call | tf_op jit(solution)/shard_map/attention/pallas_call | solution.py:81
  (13 shorter events, 0.1 us)
Async XLA Ops:
  7.2 73.9 %copy-start = (bf16[1,768,1536]{2,1,0:T(8,128)(2,1)S(1)}, bf16[1,768,1536]{2,1,0:T(8,128)(2,1)}, u32[]{:S(2)}) copy-start(bf16[1,768,1536]{2,1,0:T(8,128)(2,1)} %param.17) | copy-start | bytes 7077892
  7.2 64.2 %all-gather.4.cloned.1.call-start = ((), (), s32[]{:S(2)}) async-start(), calls=%async_computation.1 | async-start | bytes 6684672 | tf_op jit(solution)/shard_map/all_gather | solution.py:117
  7.9 164.3 %reduce-scatter.2.cloned.1.call-start = ((), (), s32[]{:S(2)}) async-start(), calls=%async_computation.2 | async-start | bytes 6684672 | tf_op jit(solution)/shard_map/reduce_scatter | solution.py:144
  71.4 3.9 %copy-start.3 = (bf16[1,1536,768]{2,1,0:T(8,128)(2,1)S(1)}, bf16[1,1536,768]{2,1,0:T(8,128)(2,1)}, u32[]{:S(2)}) copy-start(bf16[1,1536,768]{2,1,0:T(8,128)(2,1)} %param.16) | copy-start | bytes 7077892
  75.4 2.6 copy-start.4
  88.5 83.8 %copy-start.2 = (bf16[128,1536]{1,0:T(8,128)(2,1)S(1)}, bf16[128,1536]{1,0:T(8,128)(2,1)}, u32[]{:S(2)}) copy-start(bf16[128,1536]{1,0:T(8,128)(2,1)} %param.11) | copy-start | bytes 1179652
  88.5 157.0 %copy-start.5 = (f32[1536]{0:T(1024)S(1)}, f32[1536]{0:T(1024)}, u32[]{:S(2)}) copy-start(f32[1536]{0:T(1024)} %param.18) | copy-start | bytes 18436
  88.5 159.7 %copy-start.6 = (s32[1,6]{1,0:T(1,128)S(1)}, s32[1,6]{1,0:T(1,128)}, u32[]{:S(2)}) copy-start(s32[1,6]{1,0:T(1,128)} %param.14) | copy-start | bytes 76
  88.5 157.0 %all-gather.6.cloned.1.call-start = ((), (), s32[]{:S(2)}) async-start(), calls=%async_computation.3 | async-start | bytes 8355840 | tf_op jit(solution)/shard_map/all_gather | solution.py:118
  89.3 199.2 %all-gather.8.cloned.1.call-start = ((), (), s32[]{:S(2)}) async-start(), calls=%async_computation.4 | async-start | bytes 2228224 | tf_op jit(solution)/shard_map/all_gather | solution.py:151
  288.5 1.6 copy-start.1
Sparse Core Ops, SparseCore 0:
  10.3 61.0 all-gather.3
  88.6 83.5 reduce-scatter.1
  174.8 70.6 all-gather.5
  248.4 40.0 all-gather.7

commit v2 on v1

--- a/solution.py
+++ b/solution.py
@@ -94,6 +94,339 @@
     )(qt, kv)
 
 
+MESH = pl.DeviceIdType.MESH
+
+
+def position():
+    me = lax.axis_index("seq")
+    return me, me // 4, (me // 2) % 2, me % 2
+
+
+def at(z, y, c):
+    return (z * 2 + y) * 2 + c
+
+
+def remote(src, dst, send_sem, recv_sem, target):
+    return pltpu.make_async_remote_copy(
+        src_ref=src,
+        dst_ref=dst,
+        send_sem=send_sem,
+        recv_sem=recv_sem,
+        device_id={"seq": target},
+        device_id_type=MESH,
+    )
+
+
+def greet(rows):
+    me, z, y, c = position()
+    barrier = pltpu.get_barrier_semaphore()
+    near = (
+        at((z + 1) % rows, y, c),
+        at((z + rows - 1) % rows, y, c),
+        at(z, 1 - y, c),
+        at(z, y, 1 - c),
+    )
+    for target in near:
+        pl.semaphore_signal(barrier, inc=1, device_id={"seq": target}, device_id_type=MESH)
+    pl.semaphore_wait(barrier, len(near))
+
+
+def gather_kernel(rows, streams, *refs):
+    n = len(streams)
+    ins, outs = refs[:n], refs[n : 2 * n]
+    local_sem, recv_sem, z_sem, y_sem, c_sem = refs[2 * n :]
+    me, z, y, c = position()
+    last = rows - 1
+    for i in range(n):
+        pltpu.make_async_copy(ins[i], outs[i].at[me], local_sem.at[i]).start()
+    greet(rows)
+    parts = []
+    for i, (width, cut) in enumerate(streams):
+        parts.append((i, slice(0, cut), True))
+        if cut < width:
+            parts.append((i, slice(cut, width), False))
+
+    def copies(k, zz, yy, cc, own):
+        i, cols, _ = parts[k]
+        block = at(zz, yy, cc)
+        src = ins[i].at[:, cols] if own else outs[i].at[block, :, cols]
+        dst = outs[i].at[block, :, cols]
+        got = recv_sem.at[k, block]
+        line = zz * 2 + yy
+        return {
+            "up": lambda: remote(src, dst, z_sem.at[k, 0, line], got, at(lax.rem(z + 1, rows), y, c)),
+            "down": lambda: remote(
+                src, dst, z_sem.at[k, 1, line], got, at(lax.rem(z + last, rows), y, c)
+            ),
+            "y": lambda: remote(src, dst, y_sem.at[k, line], got, at(z, 1 - y, c)),
+            "core": lambda: remote(src, dst, c_sem.at[k, line], got, at(z, y, 1 - c)),
+        }
+
+    def await_block(k, zz, yy, cc):
+        copies(k, zz, yy, cc, False)["core"]().wait_recv()
+
+    def act(verb, k, zz, yy, own, up, down, across):
+        made = copies(k, zz, yy, c, own)
+        if up:
+            pl.when(z < last)(lambda: getattr(made["up"](), verb)())
+        if down:
+            pl.when(z > 0)(lambda: getattr(made["down"](), verb)())
+        if across:
+            getattr(made["y"](), verb)()
+        getattr(made["core"](), verb)()
+
+    pass_on = functools.partial(act, "start")
+    finish = functools.partial(act, "wait_send")
+
+    def walk(action, waiting):
+        for k, (_, _, z_first) in enumerate(parts):
+            action(k, z, y, True, True, True, True)
+        for k, (_, _, z_first) in enumerate(parts):
+            if not z_first:
+                if waiting:
+                    await_block(k, z, 1 - y, c)
+                action(k, z, 1 - y, False, True, True, False)
+        for step in range(1, rows):
+            for k, (_, _, z_first) in enumerate(parts):
+                for yy in (y,) if z_first else (y, 1 - y):
+
+                    @pl.when(z - step >= 0)
+                    def _():
+                        if waiting:
+                            await_block(k, z - step, yy, c)
+                        action(k, z - step, yy, False, True, False, z_first)
+
+                    @pl.when(z + step < rows)
+                    def _():
+                        if waiting:
+                            await_block(k, z + step, yy, c)
+                        action(k, z + step, yy, False, False, True, z_first)
+
+            for k, (_, _, z_first) in enumerate(parts):
+                if z_first:
+
+                    def hand(zz):
+                        if waiting:
+                            await_block(k, zz, 1 - y, c)
+                        action(k, zz, 1 - y, False, False, False, False)
+
+                    if step == 1:
+                        hand(z)
+                    else:
+                        pl.when(z - step + 1 >= 0)(lambda: hand(z - step + 1))
+                        pl.when(z + step - 1 < rows)(lambda: hand(z + step - 1))
+        for k, (_, _, z_first) in enumerate(parts):
+            if z_first:
+                pl.when(z - last >= 0)(lambda: hand_last(k, z - last, waiting, action))
+                pl.when(z + last < rows)(lambda: hand_last(k, z + last, waiting, action))
+
+    def hand_last(k, zz, waiting, action):
+        if waiting:
+            await_block(k, zz, 1 - y, c)
+        action(k, zz, 1 - y, False, False, False, False)
+
+    walk(pass_on, True)
+    for k in range(len(parts)):
+        for zz in range(rows):
+            for yy in range(2):
+                await_block(k, zz, yy, 1 - c)
+    walk(finish, False)
+    for i in range(n):
+        pltpu.make_async_copy(ins[i], outs[i].at[me], local_sem.at[i]).wait()
+
+
+def gather(arrays, cuts, seq, collective_id, name):
+    streams = tuple((a.shape[1], cut) for a, cut in zip(arrays, cuts))
+    k = sum(1 if cut >= width else 2 for width, cut in streams)
+    rows = seq // 4
+    dma = pltpu.SemaphoreType.DMA
+    return pl.pallas_call(
+        functools.partial(gather_kernel, rows, streams),
+        out_shape=[jax.ShapeDtypeStruct((seq,) + a.shape, a.dtype) for a in arrays],
+        in_specs=[pl.BlockSpec(memory_space=pltpu.VMEM)] * len(arrays),
+        out_specs=[pl.BlockSpec(memory_space=pltpu.VMEM)] * len(arrays),
+        scratch_shapes=[
+            dma((len(arrays),)),
+            dma((k, seq)),
+            dma((k, 2, 2 * rows)),
+            dma((k, 2 * rows)),
+            dma((k, 2 * rows)),
+        ],
+        compiler_params=pltpu.CompilerParams(
+            collective_id=collective_id, has_side_effects=True, vmem_limit_bytes=48 * 1024 * 1024
+        ),
+        cost_estimate=pl.CostEstimate(flops=0, bytes_accessed=100_000_000, transcendentals=0),
+        name=name,
+    )(*arrays)
+
+
+def scatter_kernel(
+    rows, part_ref, res_ref, gain_ref, out_ref, acc, c_buf, ya_buf, za_buf, zb_buf, yb_buf, mix,
+    cs, cr, yas, yar, zas, zar, zbs, zbr, ybs, ybr,
+):
+    me, z, y, c = position()
+    last = rows - 1
+    half = part_ref.shape[2] // 2
+    left, right = slice(0, half), slice(half, 2 * half)
+    above, below = lax.rem(z + 1, rows), lax.rem(z + last, rows)
+    other_y, other_c = at(z, 1 - y, c), at(z, y, 1 - c)
+    greet(rows)
+    order = []
+    for i in range((rows + 1) // 2):
+        order += [i] if i == last - i else [i, last - i]
+
+    def core_copy(zz, yy):
+        line = zz * 2 + yy
+        return remote(part_ref.at[at(zz, yy, 1 - c)], c_buf.at[line], cs.at[line], cr.at[line], other_c)
+
+    def ya_copy(zz):
+        return remote(acc.at[zz * 2 + 1 - y, :, left], ya_buf.at[zz], yas.at[zz], yar.at[zz], other_y)
+
+    def yb_copy():
+        return remote(acc.at[z * 2 + 1 - y, :, right], yb_buf, ybs, ybr, other_y)
+
+    def za_copy(zz, way):
+        target = at(above if way == 0 else below, y, c)
+        return remote(acc.at[zz * 2 + y, :, left], za_buf.at[way, zz], zas.at[zz], zar.at[way, zz], target)
+
+    def zb_copy(zz, yy, way):
+        target = at(above if way == 0 else below, y, c)
+        line = zz * 2 + yy
+        return remote(acc.at[line, :, right], zb_buf.at[way, line], zbs.at[line], zbr.at[way, line], target)
+
+    def add(line, cols, value):
+        acc[line, :, cols] = (acc[line, :, cols].astype(F32) + value.astype(F32)).astype(BF16)
+
+    for zz in order:
+        for yy in (1 - y, y):
+            core_copy(zz, yy).start()
+    for zz in order:
+        for yy in (1 - y, y):
+            line = zz * 2 + yy
+            core_copy(zz, yy).wait_recv()
+            acc[line] = (part_ref[at(zz, yy, c)].astype(F32) + c_buf[line].astype(F32)).astype(BF16)
+            if zz < last:
+                pl.when(z == last)(lambda: zb_copy(zz, yy, 1).start())
+            if zz > 0:
+                pl.when(z == 0)(lambda: zb_copy(zz, yy, 0).start())
+        ya_copy(zz).start()
+    for zz in order:
+
+        def add_za(way):
+            za_copy(zz, way).wait_recv()
+            add(zz * 2 + y, left, za_buf[way, zz])
+
+        def add_zb(yy, way):
+            zb_copy(zz, yy, way).wait_recv()
+            add(zz * 2 + yy, right, zb_buf[way, zz * 2 + yy])
+
+        for yy in (1 - y, y):
+
+            @pl.when((z > zz) & (z < last))
+            def _():
+                add_zb(yy, 1)
+                zb_copy(zz, yy, 1).start()
+
+            @pl.when((z < zz) & (z > 0))
+            def _():
+                add_zb(yy, 0)
+                zb_copy(zz, yy, 0).start()
+
+        ya_copy(zz).wait_recv()
+        add(zz * 2 + y, left, ya_buf[zz])
+
+        @pl.when(z > zz)
+        def _():
+            pl.when(z < last)(lambda: add_za(1))
+            za_copy(zz, 1).start()
+
+        @pl.when(z < zz)
+        def _():
+            pl.when(z > 0)(lambda: add_za(0))
+            za_copy(zz, 0).start()
+
+    for yy in (1 - y, y):
+        line = z * 2 + yy
+
+        @pl.when(z < last)
+        def _():
+            zb_copy(z, yy, 1).wait_recv()
+            add(line, right, zb_buf[1, line])
+
+        @pl.when(z > 0)
+        def _():
+            zb_copy(z, yy, 0).wait_recv()
+            add(line, right, zb_buf[0, line])
+
+    yb_copy().start()
+    mine = z * 2 + y
+    mix[:, left] = res_ref[:, left].astype(F32) + acc[mine, :, left].astype(F32)
+
+    @pl.when(z < last)
+    def _():
+        za_copy(z, 1).wait_recv()
+        mix[:, left] += za_buf[1, z].astype(F32)
+
+    @pl.when(z > 0)
+    def _():
+        za_copy(z, 0).wait_recv()
+        mix[:, left] += za_buf[0, z].astype(F32)
+
+    yb_copy().wait_recv()
+    mix[:, right] = res_ref[:, right].astype(F32) + (
+        acc[mine, :, right].astype(F32) + yb_buf[...].astype(F32)
+    )
+    mixed = mix[...]
+    scale = lax.rsqrt(jnp.mean(mixed * mixed, axis=-1, keepdims=True) + 1e-05)
+    out_ref[...] = (mixed * scale * gain_ref[...]).astype(BF16)
+    for zz in range(rows):
+        for yy in range(2):
+            core_copy(zz, yy).wait_send()
+            pl.when(z > zz)(lambda: zb_copy(zz, yy, 1).wait_send())
+            pl.when(z < zz)(lambda: zb_copy(zz, yy, 0).wait_send())
+        ya_copy(zz).wait_send()
+        pl.when(z > zz)(lambda: za_copy(zz, 1).wait_send())
+        pl.when(z < zz)(lambda: za_copy(zz, 0).wait_send())
+    yb_copy().wait_send()
+
+
+def scatter_norm(partial, residual, gain, seq):
+    _, tokens, width = partial.shape
+    rows = seq // 4
+    half = width // 2
+    dma = pltpu.SemaphoreType.DMA
+    return pl.pallas_call(
+        functools.partial(scatter_kernel, rows),
+        out_shape=jax.ShapeDtypeStruct((tokens, width), BF16),
+        in_specs=[pl.BlockSpec(memory_space=pltpu.VMEM)] * 3,
+        out_specs=pl.BlockSpec(memory_space=pltpu.VMEM),
+        scratch_shapes=[
+            pltpu.VMEM((2 * rows, tokens, width), BF16),
+            pltpu.VMEM((2 * rows, tokens, width), BF16),
+            pltpu.VMEM((rows, tokens, half), BF16),
+            pltpu.VMEM((2, rows, tokens, half), BF16),
+            pltpu.VMEM((2, 2 * rows, tokens, half), BF16),
+            pltpu.VMEM((tokens, half), BF16),
+            pltpu.VMEM((tokens, width), F32),
+            dma((2 * rows,)),
+            dma((2 * rows,)),
+            dma((rows,)),
+            dma((rows,)),
+            dma((rows,)),
+            dma((2, rows)),
+            dma((2 * rows,)),
+            dma((2, 2 * rows)),
+            dma,
+            dma,
+        ],
+        compiler_params=pltpu.CompilerParams(
+            collective_id=2, has_side_effects=True, vmem_limit_bytes=48 * 1024 * 1024
+        ),
+        cost_estimate=pl.CostEstimate(flops=0, bytes_accessed=100_000_000, transcendentals=0),
+        name="scatter_norm",
+    )(partial, residual, gain.reshape(1, width))
+
+
 def on_device(
     moe_input,
     residual_in,
@@ -112,20 +445,19 @@
     cap = min(tokens, max(2, tokens * TOP * 2 // seq))
     raised = jnp.exp(route_logits)
     weights = raised / jnp.sum(raised, axis=-1, keepdims=True)
-    meta = jnp.concatenate([expert_ids.astype(F32), weights], axis=1)
-    meta = lax.all_gather(meta, "seq", axis=0, tiled=True)
-    rows = lax.all_gather(moe_input, "seq", axis=0, tiled=True)
+    meta = jnp.concatenate([expert_ids.astype(F32), weights], axis=1).T
     qkv_full = lax.all_gather(qkv_weight, "seq", axis=0, tiled=True)
+    rows, meta = gather((moe_input, meta), (width // 2, tokens), seq, 0, "gather_tokens")
 
     hit = (meta[:, :TOP] == me.astype(F32)).astype(F32)
-    share = jnp.sum(hit * meta[:, TOP:], axis=1).reshape(seq, tokens)
-    named = jnp.sum(hit, axis=1).reshape(seq, tokens)
+    share = jnp.sum(hit * meta[:, TOP:], axis=1)
+    named = jnp.sum(hit, axis=1)
     earlier = (jnp.arange(tokens)[:, None] < jnp.arange(tokens)[None, :]).astype(F32)
     slot = jnp.dot(named, earlier)
     slot = jnp.where(named > 0.5, slot, -1.0)
     place = (slot[:, None, :] == jnp.arange(cap, dtype=F32)[None, :, None]).astype(BF16)
     sent = jnp.einsum(
-        "sct,std->scd", place, rows.reshape(seq, tokens, width), preferred_element_type=F32
+        "sct,std->scd", place, rows, preferred_element_type=F32
     ).astype(BF16).reshape(seq * cap, width)
     gate_part = jnp.dot(sent, w_gate[0], preferred_element_type=F32)
     up_part = jnp.dot(sent, w_up[0], preferred_element_type=F32)
@@ -140,15 +472,21 @@
     back = jnp.einsum(
         "sct,scd->std", place, result.reshape(seq, cap, width), preferred_element_type=F32
     )
-    partial = (back * share[..., None]).astype(BF16).reshape(seq * tokens, width)
-    moe = lax.psum_scatter(partial, "seq", scatter_dimension=0, tiled=True)
-    mixed = residual_in.astype(F32) + moe.astype(F32)
-    normed = (
-        mixed * lax.rsqrt(jnp.mean(mixed * mixed, axis=-1, keepdims=True) + 1e-05) * norm_gain
-    ).astype(BF16)
+    partial = (back * share[..., None]).astype(BF16)
+    if seq <= 16:
+        normed = scatter_norm(partial, residual_in, norm_gain, seq)
+    else:
+        moe = lax.psum_scatter(
+            partial.reshape(seq * tokens, width), "seq", scatter_dimension=0, tiled=True
+        )
+        mixed = residual_in.astype(F32) + moe.astype(F32)
+        normed = (
+            mixed * lax.rsqrt(jnp.mean(mixed * mixed, axis=-1, keepdims=True) + 1e-05) * norm_gain
+        ).astype(BF16)
     query_width = QH * HD
     keys_vals = jnp.dot(normed, qkv_full[:, query_width:], preferred_element_type=F32).astype(BF16)
-    kv = lax.all_gather(keys_vals, "seq", axis=0, tiled=True)
+    (kv,) = gather((keys_vals,), (KVH * HD,), seq, 1, "gather_kv")
+    kv = kv.reshape(seq * tokens, 2 * KVH * HD)
     queries = jnp.dot(normed, qkv_full[:, :query_width], preferred_element_type=F32).astype(BF16)
     attention = attention_call((queries * HD ** (-0.5)).T, kv)
     return (attention, neuron_energy)

time: 319 us -> 256 us (0.80)
  waiting for transfers between devices: 234 us -> 0.7 us
  Pallas kernels: 22.5 us -> 211 us
  blocking collectives: 17.2 us -> 0 us
    pallas_call x0 -> x3, Pallas kernels: none -> 189 us  [the longest x2 127 us: gather(): pl.pallas_call(functools.partial(gather_kernel, rows, streams), out_shape...]
    reduce_scatter x1 -> x0, waiting for transfers between devices: 82.8 us -> none  [on_device(): moe = lax.psum_scatter(partial, 'seq', scatter_dimension=0, tiled=True)]
    all_gather x2 -> x0, waiting for transfers between devices: 77.8 us -> none  [the longest x1 43.9 us: on_device(): rows = lax.all_gather(moe_input, 'seq', axis=0, tiled=True)]
    all_gather x1, waiting for transfers between devices: 72.1 us -> 0.02 us  [on_device(): qkv_full = lax.all_gather(qkv_weight, 'seq', axis=0, tiled=True)]
    all_gather x1 -> x0, blocking collectives: 17.2 us -> none  [on_device(): meta = lax.all_gather(meta, 'seq', axis=0, tiled=True)]
  transfers between devices with their start and end apart: 4 -> 1, of which waited for: 4 -> 0; matrix products, arithmetic and copies ran while one was open for 3% -> 8% of each run, Pallas kernels for 0% -> 62%
where the time goes in v2:
time: 256 us; the launch traced here: 255 us
  Pallas kernels  211 us (82%)
  matrix products  24.5 us (10%)
  between operations  14.2 us (6%)
    pallas_call x2, Pallas kernels, gather(): pl.pallas_call(functools.partial(gather_kernel, rows, streams), out_shape...  127 us
    pallas_call x1, Pallas kernels, scatter_norm(): pl.pallas_call(functools.partial(scatter_kernel, rows), out_shape=jax.Sha...  62 us
    pallas_call x1, Pallas kernels, attention_call(): pl.pallas_call(attention_kernel, out_shape=jax.ShapeDtypeStruct((tokens,...  22.5 us
    dot_general x1, matrix products, on_device(): jnp.dot(normed, qkv_full[:, :query_width], preferred_element_type=F32)  5.34 us
  transfers between devices with their start and end apart: 1, of which 0 were waited for; matrix products, arithmetic and copies ran while one was open for 8% of the time, Pallas kernels for 62%

profile of v2, /device:TPU:29, one launch (start us, length us, event | category | flops | bytes accessed | tf_op | source)
XLA Modules:
  0.0 255.2 jit_solution(17934408984955764565)
XLA Ops:
  7.2 0.0 copy-start
  7.2 0.0 all-gather.2.cloned.1.call-start
  7.2 0.7 all-gather.2.cloned.1.call-update
  7.9 0.7 convert_element_type.32
  8.6 0.7 reshape.32.gain_ref
  9.3 0.7 exponential_reduce_fusion
  10.0 0.7 exponential_divide_fusion
  10.7 0.0 copy-start.2
  10.7 1.0 copy-done.2
  11.7 95.8 %gather_tokens.1 = (bf16[16,128,1536]{2,1,0:T(8,128)(2,1)}, f32[16,8,128]{2,1,0:T(8,128)S(1)}) custom-call(bf16[128,1536]{1,0:T(8,128)(2,1)S(1)} %copy-done.2, f32[8,128]{1,0:T(8,128)S(1)} %maximum_bitcast_fusion.refs_1_), custom_call_target="tpu_custom_call" | custom-call | bytes 100000000 | tf_op jit(solution)/shard_map/gather_tokens/pallas_call | solution.py:243
  107.6 0.1 convolution_select_fusion
  107.7 3.9 %convolution_convert_fusion.1 = bf16[16,64,1536]{2,1,0:T(8,128)(2,1)S(1)} fusion(bf16[16,128,1536]{2,1,0:T(8,128)(2,1)} %get-tuple-element.5, f32[16,128]{1,0:T(8,128)S(1)} %convolution_select_fusion), kind=kOutput, calls=%fused_computation.4 | convolution fusion | flops 404357120 | bytes 9445376 | tf_op jit(solution)/shard_map/sct,std->scd/dot_general | solution.py:459
  111.6 0.0 copy-done.3
  111.6 0.0 copy-start.4
  111.6 2.6 %fusion.6 = f32[1024,768]{1,0:T(8,128)S(1)} fusion(bf16[1024,1536]{1,0:T(8,128)(2,1)S(1)} %bitcast.39, bf16[1,1536,768]{2,1,0:T(8,128)(2,1)S(1)} %copy-done.3), kind=kOutput, calls=%fused_computation.9 | convolution fusion | flops 2415919104 | bytes 8650752 | tf_op jit(solution)/shard_map/dot_general | solution.py:463
  114.2 0.0 copy-done.4
  114.3 0.0 copy-start.5
  114.3 3.1 %multiply_reduce_fusion = (f32[768]{0:T(1024)S(1)}, bf16[1024,768]{1,0:T(8,128)(2,1)S(1)}) fusion(f32[1024,768]{1,0:T(8,128)S(1)} %fusion.6, bf16[1024,1536]{1,0:T(8,128)(2,1)S(1)} %bitcast.40, bf16[1,1536,768]{2,1,0:T(8,128)(2,1)S(1)} %copy-done.4), kind=kOutput, calls=%fused_computation.5 | convolution fusion | flops 2422209792 | bytes 10226688 | tf_op jit(solution)/shard_map/dot_general | solution.py:462
  117.3 0.0 copy-done.5
  117.4 0.3 convolution_bitcast_fusion
  117.6 0.6 copy.16
  118.2 0.0 copy-done
  118.2 2.8 %convolution_convert_fusion = bf16[1024,1536]{1,0:T(8,128)(2,1)S(1)} fusion(bf16[1,768,1536]{2,1,0:T(8,128)(2,1)S(1)} %copy-done, bf16[1024,768]{1,0:T(8,128)(2,1)S(1)} %get-tuple-element.9), kind=kOutput, calls=%fused_computation.3 | convolution fusion | flops 2417491968 | bytes 7077888 | tf_op jit(solution)/shard_map/dot_general | solution.py:466
  121.0 0.0 copy-start.1
  121.1 4.6 %multiply_convert_fusion.part_ref = bf16[16,128,1536]{2,1,0:T(8,128)(2,1)} fusion(bf16[16,64,1536]{2,1,0:T(8,128)(2,1)S(1)} %bitcast.41, f32[16,128]{1,0:T(8,128)S(1)} %get-tuple-element.6, f32[16,128]{1,0:T(8,128)S(1)} %convolution_select_fusion), kind=kOutput, calls=%fused_computation | convolution fusion | flops 409075712 | bytes 9453568 | tf_op jit(solution)/shard_map/sct,scd->std/dot_general | solution.py:472
  125.7 0.0 copy-done.1
  125.7 62.0 %scatter_norm.1 = bf16[128,1536]{1,0:T(8,128)(2,1)S(1)} custom-call(bf16[16,128,1536]{2,1,0:T(8,128)(2,1)} %multiply_convert_fusion.part_ref, bf16[128,1536]{1,0:T(8,128)(2,1)S(1)} %copy-done.1, f32[1,1536]{1,0:T(1,128)S(1)} %reshape.32.gain_ref), custom_call_target="tpu_custom_call" | custom-call | bytes 100000000 | tf_op jit(solution)/shard_map/scatter_norm/pallas_call | solution.py:398
  187.6 0.0 all-gather.2.cloned.1.call-done
  187.7 1.8 fusion.21.refs_0_
  189.5 31.0 %gather_kv.1 = bf16[16,128,512]{2,1,0:T(8,128)(2,1)S(1)} custom-call(bf16[128,512]{1,0:T(8,128)(2,1)S(1)} %fusion.21.refs_0_), custom_call_target="tpu_custom_call" | custom-call | bytes 100000000 | tf_op jit(solution)/shard_map/gather_kv/pallas_call | solution.py:243
  220.5 5.3 %fusion.13.qt_ref = bf16[2048,128]{1,0:T(8,128)(2,1)S(1)} fusion(bf16[128,1536]{1,0:T(8,128)(2,1)S(1)} %scatter_norm.1, bf16[1536,2560]{1,0:T(8,128)(2,1)} %all-gather.2.cloned.1.call-done), kind=kOutput, calls=%fused_computation.14 | convolution fusion | flops 805830656 | bytes 7208960 | tf_op jit(solution)/shard_map/dot_general | solution.py:490
  225.8 22.5 %attention.1 = bf16[128,2048]{1,0:T(8,128)(2,1)} custom-call(bf16[2048,128]{1,0:T(8,128)(2,1)S(1)} %fusion.13.qt_ref, bf16[2048,512]{1,0:T(8,128)(2,1)S(1)} %bitcast.38), custom_call_target="tpu_custom_call" | custom-call | tf_op jit(solution)/shard_map/attention/pallas_call | solution.py:81
  (3 shorter events, 0.1 us)
Async XLA Ops:
  7.2 111.1 %copy-start = (bf16[1,768,1536]{2,1,0:T(8,128)(2,1)S(1)}, bf16[1,768,1536]{2,1,0:T(8,128)(2,1)}, u32[]{:S(2)}) copy-start(bf16[1,768,1536]{2,1,0:T(8,128)(2,1)} %param.17) | copy-start | bytes 7077892
  7.2 180.5 %all-gather.2.cloned.1.call-start = ((), (), s32[]{:S(2)}) async-start(), calls=%async_computation | async-start | bytes 8355840 | tf_op jit(solution)/shard_map/all_gather | solution.py:449
  10.7 1.0 copy-start.2
  107.7 3.9 %copy-start.3 = (bf16[1,1536,768]{2,1,0:T(8,128)(2,1)S(1)}, bf16[1,1536,768]{2,1,0:T(8,128)(2,1)}, u32[]{:S(2)}) copy-start(bf16[1,1536,768]{2,1,0:T(8,128)(2,1)} %param.16) | copy-start | bytes 7077892
  111.6 2.6 %copy-start.4 = (bf16[1,1536,768]{2,1,0:T(8,128)(2,1)S(1)}, bf16[1,1536,768]{2,1,0:T(8,128)(2,1)}, u32[]{:S(2)}) copy-start(bf16[1,1536,768]{2,1,0:T(8,128)(2,1)} %param.15) | copy-start | bytes 7077892
  114.3 3.1 %copy-start.5 = (s32[1,6]{1,0:T(1,128)S(1)}, s32[1,6]{1,0:T(1,128)}, u32[]{:S(2)}) copy-start(s32[1,6]{1,0:T(1,128)} %param.14) | copy-start | bytes 76
  121.0 4.6 %copy-start.1 = (bf16[128,1536]{1,0:T(8,128)(2,1)S(1)}, bf16[128,1536]{1,0:T(8,128)(2,1)}, u32[]{:S(2)}) copy-start(bf16[128,1536]{1,0:T(8,128)(2,1)} %res_ref.1) | copy-start | bytes 1179652
Sparse Core Ops, SparseCore 0:
  10.3 92.3 all-gather.1

commit v3 on v2

--- a/solution.py
+++ b/solution.py
@@ -131,20 +131,29 @@
     pl.semaphore_wait(barrier, len(near))
 
 
-def gather_kernel(rows, streams, *refs):
-    n = len(streams)
-    ins, outs = refs[:n], refs[n : 2 * n]
-    local_sem, recv_sem, z_sem, y_sem, c_sem = refs[2 * n :]
+def experts_kernel(
+    rows, cap, x_ref, meta_ref, wq_ref, wg_ref, wu_ref, wd_ref,
+    part_ref, energy_ref, wq_out, x_all, meta_all, sent, place_scr, local_sem, recv_sem, z_sem, y_sem, c_sem,
+):
     me, z, y, c = position()
     last = rows - 1
-    for i in range(n):
-        pltpu.make_async_copy(ins[i], outs[i].at[me], local_sem.at[i]).start()
+    tokens, width = x_ref.shape
+    half, whalf = width // 2, wq_ref.shape[1] // 2
+    ins, outs = (x_ref, meta_ref, wq_ref), (x_all, meta_all, wq_out)
+    parts = (
+        (0, slice(0, half), True),
+        (0, slice(half, width), False),
+        (1, slice(0, tokens), True),
+        (2, slice(0, whalf), True),
+        (2, slice(whalf, 2 * whalf), False),
+    )
+
+    def own_copy(i):
+        return pltpu.make_async_copy(ins[i], outs[i].at[me], local_sem.at[i])
+
+    for i in range(3):
+        own_copy(i).start()
     greet(rows)
-    parts = []
-    for i, (width, cut) in enumerate(streams):
-        parts.append((i, slice(0, cut), True))
-        if cut < width:
-            parts.append((i, slice(cut, width), False))
 
     def copies(k, zz, yy, cc, own):
         i, cols, _ = parts[k]
@@ -175,89 +184,142 @@
             getattr(made["y"](), verb)()
         getattr(made["core"](), verb)()
 
-    pass_on = functools.partial(act, "start")
-    finish = functools.partial(act, "wait_send")
-
-    def walk(action, waiting):
-        for k, (_, _, z_first) in enumerate(parts):
-            action(k, z, y, True, True, True, True)
-        for k, (_, _, z_first) in enumerate(parts):
-            if not z_first:
-                if waiting:
-                    await_block(k, z, 1 - y, c)
-                action(k, z, 1 - y, False, True, True, False)
-        for step in range(1, rows):
-            for k, (_, _, z_first) in enumerate(parts):
+    def pass_on(*args):
+        act("start", *args)
+
+    def finish(*args):
+        act("wait_send", *args)
+
+    def walk_step(chosen, step, action, waiting):
+        def reached(k, zz, yy, up, down, across):
+            if waiting:
+                await_block(k, zz, yy, c)
+            action(k, zz, yy, False, up, down, across)
+
+        if step == 0:
+            for k in chosen:
+                action(k, z, y, True, True, True, True)
+            return
+        if step == 1:
+            for k in chosen:
+                if not parts[k][2]:
+                    reached(k, z, 1 - y, True, True, False)
+        if step < rows:
+            for k in chosen:
+                z_first = parts[k][2]
                 for yy in (y,) if z_first else (y, 1 - y):
 
                     @pl.when(z - step >= 0)
                     def _():
-                        if waiting:
-                            await_block(k, z - step, yy, c)
-                        action(k, z - step, yy, False, True, False, z_first)
+                        reached(k, z - step, yy, True, False, z_first)
 
                     @pl.when(z + step < rows)
                     def _():
-                        if waiting:
-                            await_block(k, z + step, yy, c)
-                        action(k, z + step, yy, False, False, True, z_first)
-
-            for k, (_, _, z_first) in enumerate(parts):
-                if z_first:
-
-                    def hand(zz):
-                        if waiting:
-                            await_block(k, zz, 1 - y, c)
-                        action(k, zz, 1 - y, False, False, False, False)
-
-                    if step == 1:
-                        hand(z)
-                    else:
-                        pl.when(z - step + 1 >= 0)(lambda: hand(z - step + 1))
-                        pl.when(z + step - 1 < rows)(lambda: hand(z + step - 1))
-        for k, (_, _, z_first) in enumerate(parts):
-            if z_first:
-                pl.when(z - last >= 0)(lambda: hand_last(k, z - last, waiting, action))
-                pl.when(z + last < rows)(lambda: hand_last(k, z + last, waiting, action))
-
-    def hand_last(k, zz, waiting, action):
-        if waiting:
-            await_block(k, zz, 1 - y, c)
-        action(k, zz, 1 - y, False, False, False, False)
-
-    walk(pass_on, True)
-    for k in range(len(parts)):
-        for zz in range(rows):
-            for yy in range(2):
-                await_block(k, zz, yy, 1 - c)
-    walk(finish, False)
-    for i in range(n):
-        pltpu.make_async_copy(ins[i], outs[i].at[me], local_sem.at[i]).wait()
-
-
-def gather(arrays, cuts, seq, collective_id, name):
-    streams = tuple((a.shape[1], cut) for a, cut in zip(arrays, cuts))
-    k = sum(1 if cut >= width else 2 for width, cut in streams)
+                        reached(k, z + step, yy, False, True, z_first)
+
+        for k in chosen:
+            if parts[k][2]:
+                if step == 1:
+                    reached(k, z, 1 - y, False, False, False)
+                else:
+
+                    @pl.when(z - step + 1 >= 0)
+                    def _():
+                        reached(k, z - step + 1, 1 - y, False, False, False)
+
+                    @pl.when(z + step - 1 < rows)
+                    def _():
+                        reached(k, z + step - 1, 1 - y, False, False, False)
+
+    def from_core(chosen):
+        for k in chosen:
+            for zz in range(rows):
+                for yy in range(2):
+                    await_block(k, zz, yy, 1 - c)
+
+    first, second = (2, 0, 1), (3, 4)
+    for step in range(rows + 1):
+        walk_step(first, step, pass_on, True)
+    walk_step(second, 0, pass_on, True)
+    from_core(first)
+    own_copy(0).wait()
+    own_copy(1).wait()
+
+    batch = 2 * 2
+    earlier = (
+        lax.broadcasted_iota(jnp.int32, (tokens, tokens), 0)
+        < lax.broadcasted_iota(jnp.int32, (tokens, tokens), 1)
+    ).astype(F32).astype(BF16)
+    slots = lax.broadcasted_iota(jnp.int32, (cap, tokens), 0).astype(F32)
+    mine = me.astype(F32)
+    energy_ref[...] = jnp.zeros_like(energy_ref)
+    for b in range(rows):
+        shares = []
+        for i in range(batch):
+            block = b * batch + i
+            meta = meta_all[block]
+            hit = jnp.where(meta[:TOP] == mine, 1.0, 0.0)
+            named = jnp.sum(hit, axis=0, keepdims=True)
+            shares.append(jnp.sum(hit * meta[TOP:], axis=0, keepdims=True))
+            slot = jnp.dot(
+                jnp.broadcast_to(named, (16, tokens)).astype(BF16), earlier, preferred_element_type=F32
+            )[:1]
+            slot = jnp.where(named > 0.5, slot, -1.0)
+            place = jnp.where(slots == slot, 1.0, 0.0).astype(BF16)
+            place_scr[i] = place
+            sent[i * cap : (i + 1) * cap, :] = jnp.dot(
+                place, x_all[block], preferred_element_type=F32
+            ).astype(BF16)
+        gate_part = jnp.dot(sent[...], wg_ref[...], preferred_element_type=F32)
+        up_part = jnp.dot(sent[...], wu_ref[...], preferred_element_type=F32)
+        hidden = gate_part / (1.0 + jnp.exp(-gate_part)) * up_part
+        energy_ref[...] += jnp.sum(hidden * hidden, axis=0, keepdims=True)
+        result = jnp.dot(hidden.astype(BF16), wd_ref[...], preferred_element_type=F32).astype(BF16)
+        for i in range(batch):
+            back = lax.dot_general(
+                place_scr[i],
+                result[i * cap : (i + 1) * cap],
+                (((0,), (0,)), ((), ())),
+                preferred_element_type=F32,
+            )
+            share = jnp.broadcast_to(shares[i], (tokens, tokens)).T[:, :1]
+            part_ref[b * batch + i] = (back * share).astype(BF16)
+        walk_step(second, b + 1, pass_on, True)
+    from_core(second)
+    for step in range(rows + 1):
+        walk_step(first + second, step, finish, False)
+    own_copy(2).wait()
+
+
+def experts(x, meta, wq, wg, wu, wd, seq, cap):
+    tokens, width = x.shape
     rows = seq // 4
     dma = pltpu.SemaphoreType.DMA
     return pl.pallas_call(
-        functools.partial(gather_kernel, rows, streams),
-        out_shape=[jax.ShapeDtypeStruct((seq,) + a.shape, a.dtype) for a in arrays],
-        in_specs=[pl.BlockSpec(memory_space=pltpu.VMEM)] * len(arrays),
-        out_specs=[pl.BlockSpec(memory_space=pltpu.VMEM)] * len(arrays),
+        functools.partial(experts_kernel, rows, cap),
+        out_shape=[
+            jax.ShapeDtypeStruct((seq, tokens, width), BF16),
+            jax.ShapeDtypeStruct((1, wg.shape[1]), F32),
+            jax.ShapeDtypeStruct((seq,) + wq.shape, BF16),
+        ],
+        in_specs=[pl.BlockSpec(memory_space=pltpu.VMEM)] * 6,
+        out_specs=[pl.BlockSpec(memory_space=pltpu.VMEM)] * 3,
         scratch_shapes=[
-            dma((len(arrays),)),
-            dma((k, seq)),
-            dma((k, 2, 2 * rows)),
-            dma((k, 2 * rows)),
-            dma((k, 2 * rows)),
+            pltpu.VMEM((seq, tokens, width), BF16),
+            pltpu.VMEM((seq, 2 * TOP, tokens), F32),
+            pltpu.VMEM((4 * cap, width), BF16),
+            pltpu.VMEM((4, cap, tokens), BF16),
+            dma((3,)),
+            dma((5, seq)),
+            dma((5, 2, 2 * rows)),
+            dma((5, 2 * rows)),
+            dma((5, 2 * rows)),
         ],
         compiler_params=pltpu.CompilerParams(
-            collective_id=collective_id, has_side_effects=True, vmem_limit_bytes=48 * 1024 * 1024
+            collective_id=0, has_side_effects=True, vmem_limit_bytes=56 * 1024 * 1024
         ),
-        cost_estimate=pl.CostEstimate(flops=0, bytes_accessed=100_000_000, transcendentals=0),
-        name=name,
-    )(*arrays)
+        name="experts",
+    )(x, meta, wq, wg, wu, wd)
 
 
 def scatter_kernel(
@@ -427,6 +489,159 @@
     )(partial, residual, gain.reshape(1, width))
 
 
+def qkv_attention_kernel(
+    rows, n_ref, w_ref, out_ref, kv_own, kv_all, q_scr, m_scr, l_scr, acc_scr, recv_sem, z_sem, y_sem, c_sem
+):
+    me, z, y, c = position()
+    last = rows - 1
+    tokens = n_ref.shape[0]
+    query_width = QH * HD
+    heads = QCHUNK // tokens
+    chunks = QH // heads
+    greet(rows)
+    normed = n_ref[...]
+    kv_own[...] = jnp.dot(normed, w_ref[:, query_width:], preferred_element_type=F32).astype(BF16)
+
+    def place(zz, yy, cc):
+        return kv_all.at[zz * 2 + yy, pl.ds(pl.multiple_of(cc * tokens, tokens), tokens), :]
+
+    def copies(zz, yy, own):
+        src = kv_own if own else place(zz, yy, c)
+        dst = place(zz, yy, c)
+        line = zz * 2 + yy
+        got = recv_sem.at[at(zz, yy, c)]
+        return {
+            "up": lambda: remote(src, dst, z_sem.at[line], got, at(lax.rem(z + 1, rows), y, c)),
+            "y": lambda: remote(src, dst, y_sem.at[line], got, at(z, 1 - y, c)),
+            "core": lambda: remote(src, dst, c_sem.at[line], got, at(z, y, 1 - c)),
+        }
+
+    def await_block(zz, yy, cc):
+        dst = place(zz, yy, cc)
+        remote(dst, dst, c_sem.at[0], recv_sem.at[at(zz, yy, cc)], at(z, y, 1 - c)).wait_recv()
+
+    def act(verb, zz, yy, own, along):
+        made = copies(zz, yy, own)
+        if along:
+            pl.when(z < last)(lambda: getattr(made["up"](), verb)())
+            getattr(made["y"](), verb)()
+        getattr(made["core"](), verb)()
+
+    act("start", z, y, True, True)
+    kv_all[z * 2 + y, pl.ds(pl.multiple_of(c * tokens, tokens), tokens), :] = kv_own[...]
+    m_scr[...] = jnp.full_like(m_scr, -1e30)
+    l_scr[...] = jnp.zeros_like(l_scr)
+    acc_scr[...] = jnp.zeros_like(acc_scr)
+    step_cols = QCHUNK // tokens * HD
+    for ch in range(chunks):
+        q = jnp.dot(
+            normed, w_ref[:, ch * step_cols : (ch + 1) * step_cols], preferred_element_type=F32
+        )
+        q = q.astype(BF16).astype(F32) * HD ** (-0.5)
+        for h in range(0, heads, 2):
+            pair = q[:, h * HD : (h + 2) * HD].T.astype(BF16)
+            q_scr[ch, :, h * tokens : (h + 1) * tokens] = pair[:HD]
+            q_scr[ch, :, (h + 1) * tokens : (h + 2) * tokens] = pair[HD:]
+
+    def block(line, masked):
+        if masked:
+            key_pos = lax.broadcasted_iota(jnp.int32, (BK, tokens), 0)
+            query_pos = c * tokens + lax.broadcasted_iota(jnp.int32, (BK, tokens), 1)
+            hide = jnp.where(key_pos <= query_pos, 0.0, -1e30)
+            hide = jnp.concatenate([hide] * heads, axis=1)
+        for ch in range(chunks):
+            g = ch * heads // (QH // KVH)
+            keys = kv_all[line, :, g * HD : (g + 1) * HD]
+            vals = kv_all[line, :, (KVH + g) * HD : (KVH + g + 1) * HD]
+            s = jnp.dot(keys, q_scr[ch], preferred_element_type=F32)
+            if masked:
+                s = s + hide
+            m_old = m_scr[ch]
+            m_new = jnp.maximum(m_old, jnp.max(s, axis=0, keepdims=True))
+            p = jnp.exp(s - m_new)
+            alpha = jnp.exp(m_old - m_new)
+            m_scr[ch] = m_new
+            l_scr[ch] = l_scr[ch] * alpha + jnp.sum(p, axis=0, keepdims=True)
+            pv = lax.dot_general(
+                vals, p.astype(BF16), (((0,), (0,)), ((), ())), preferred_element_type=F32
+            )
+            acc_scr[ch] = acc_scr[ch] * alpha + pv
+
+    def relay(zz, yy, along):
+        await_block(zz, yy, c)
+        act("start", zz, yy, False, along)
+
+    relay(z, 1 - y, False)
+    pl.when(z >= 1)(lambda: relay(z - 1, y, True))
+    await_block(z, y, 1 - c)
+    block(z * 2 + y, True)
+    for step in range(1, rows + 1):
+        if step < last:
+            pl.when(z >= step + 1)(lambda: relay(z - step - 1, y, True))
+        if step <= last:
+            pl.when(z >= step)(lambda: relay(z - step, 1 - y, False))
+        back = step - 1
+
+        @pl.when(z >= back)
+        def _():
+            await_block(z - back, 1 - y, 1 - c)
+            if back > 0:
+                await_block(z - back, y, 1 - c)
+
+        if back == 0:
+            pl.when(y == 1)(lambda: block(z * 2, False))
+        else:
+
+            @pl.when(z >= back)
+            def _():
+                @pl.loop(0, 2)
+                def _(yy):
+                    block((z - back) * 2 + yy, False)
+
+    for ch in range(chunks):
+        o = acc_scr[ch] / l_scr[ch]
+        for h in range(0, heads, 2):
+            pair = jnp.concatenate(
+                [o[:, h * tokens : (h + 1) * tokens], o[:, (h + 1) * tokens : (h + 2) * tokens]], axis=0
+            )
+            col = (ch * heads + h) * HD
+            out_ref[:, col : col + 2 * HD] = pair.T.astype(BF16)
+    act("wait_send", z, y, True, True)
+    act("wait_send", z, 1 - y, False, False)
+    for back in range(1, rows):
+        pl.when(z >= back)(lambda: act("wait_send", z - back, y, False, True))
+        pl.when(z >= back)(lambda: act("wait_send", z - back, 1 - y, False, False))
+
+
+def qkv_attention(normed, weight, seq):
+    tokens = normed.shape[0]
+    chunks = QH * tokens // QCHUNK
+    rows = seq // 4
+    dma = pltpu.SemaphoreType.DMA
+    return pl.pallas_call(
+        functools.partial(qkv_attention_kernel, rows),
+        out_shape=jax.ShapeDtypeStruct((tokens, QH * HD), BF16),
+        in_specs=[pl.BlockSpec(memory_space=pltpu.VMEM)] * 2,
+        out_specs=pl.BlockSpec(memory_space=pltpu.VMEM),
+        scratch_shapes=[
+            pltpu.VMEM((tokens, 2 * KVH * HD), BF16),
+            pltpu.VMEM((2 * rows, 2 * tokens, 2 * KVH * HD), BF16),
+            pltpu.VMEM((chunks, HD, QCHUNK), BF16),
+            pltpu.VMEM((chunks, 1, QCHUNK), F32),
+            pltpu.VMEM((chunks, 1, QCHUNK), F32),
+            pltpu.VMEM((chunks, HD, QCHUNK), F32),
+            dma((seq,)),
+            dma((2 * rows,)),
+            dma((2 * rows,)),
+            dma((2 * rows,)),
+        ],
+        compiler_params=pltpu.CompilerParams(
+            collective_id=1, has_side_effects=True, vmem_limit_bytes=48 * 1024 * 1024
+        ),
+        name="qkv_attention",
+    )(normed, weight)
+
+
 def on_device(
     moe_input,
     residual_in,
@@ -445,48 +660,54 @@
     cap = min(tokens, max(2, tokens * TOP * 2 // seq))
     raised = jnp.exp(route_logits)
     weights = raised / jnp.sum(raised, axis=-1, keepdims=True)
-    meta = jnp.concatenate([expert_ids.astype(F32), weights], axis=1).T
+    chosen = (kept_blocks[0][:, None] == jnp.arange(OB, dtype=jnp.int32)[None, :]).astype(F32)
+
+    def unpruned(squares):
+        energy = jnp.sqrt(squares / (seq * cap) + 1e-06)
+        placed = jnp.einsum(
+            "bo,bc->oc", chosen, energy.reshape(KB, BLOCK), precision=lax.Precision.HIGHEST
+        )
+        return placed.reshape(1, OB * BLOCK)
+
+    meta = jnp.concatenate([expert_ids.astype(F32), weights], axis=1)
+    if seq == 16 and tokens == 128:
+        partial, squares, qkv_full = experts(
+            moe_input, meta.T, qkv_weight, w_gate[0], w_up[0], w_down[0], seq, cap
+        )
+        normed = scatter_norm(partial, residual_in, norm_gain, seq)
+        attention = qkv_attention(normed, qkv_full.reshape(width, -1), seq)
+        return (attention, unpruned(squares))
+    meta = lax.all_gather(meta, "seq", axis=0, tiled=True)
+    rows = lax.all_gather(moe_input, "seq", axis=0, tiled=True)
     qkv_full = lax.all_gather(qkv_weight, "seq", axis=0, tiled=True)
-    rows, meta = gather((moe_input, meta), (width // 2, tokens), seq, 0, "gather_tokens")
 
     hit = (meta[:, :TOP] == me.astype(F32)).astype(F32)
-    share = jnp.sum(hit * meta[:, TOP:], axis=1)
-    named = jnp.sum(hit, axis=1)
+    share = jnp.sum(hit * meta[:, TOP:], axis=1).reshape(seq, tokens)
+    named = jnp.sum(hit, axis=1).reshape(seq, tokens)
     earlier = (jnp.arange(tokens)[:, None] < jnp.arange(tokens)[None, :]).astype(F32)
     slot = jnp.dot(named, earlier)
     slot = jnp.where(named > 0.5, slot, -1.0)
     place = (slot[:, None, :] == jnp.arange(cap, dtype=F32)[None, :, None]).astype(BF16)
     sent = jnp.einsum(
-        "sct,std->scd", place, rows, preferred_element_type=F32
+        "sct,std->scd", place, rows.reshape(seq, tokens, width), preferred_element_type=F32
     ).astype(BF16).reshape(seq * cap, width)
     gate_part = jnp.dot(sent, w_gate[0], preferred_element_type=F32)
     up_part = jnp.dot(sent, w_up[0], preferred_element_type=F32)
     hidden = jax.nn.silu(gate_part) * up_part
-    energy = jnp.sqrt(jnp.sum(hidden * hidden, axis=0) / (seq * cap) + 1e-06)
+    neuron_energy = unpruned(jnp.sum(hidden * hidden, axis=0))
     result = jnp.dot(hidden.astype(BF16), w_down[0], preferred_element_type=F32).astype(BF16)
-    chosen = (kept_blocks[0][:, None] == jnp.arange(OB, dtype=jnp.int32)[None, :]).astype(F32)
-    placed = jnp.einsum(
-        "bo,bc->oc", chosen, energy.reshape(KB, BLOCK), precision=lax.Precision.HIGHEST
-    )
-    neuron_energy = placed.reshape(1, OB * BLOCK)
     back = jnp.einsum(
         "sct,scd->std", place, result.reshape(seq, cap, width), preferred_element_type=F32
     )
-    partial = (back * share[..., None]).astype(BF16)
-    if seq <= 16:
-        normed = scatter_norm(partial, residual_in, norm_gain, seq)
-    else:
-        moe = lax.psum_scatter(
-            partial.reshape(seq * tokens, width), "seq", scatter_dimension=0, tiled=True
-        )
-        mixed = residual_in.astype(F32) + moe.astype(F32)
-        normed = (
-            mixed * lax.rsqrt(jnp.mean(mixed * mixed, axis=-1, keepdims=True) + 1e-05) * norm_gain
-        ).astype(BF16)
+    partial = (back * share[..., None]).astype(BF16).reshape(seq * tokens, width)
+    moe = lax.psum_scatter(partial, "seq", scatter_dimension=0, tiled=True)
+    mixed = residual_in.astype(F32) + moe.astype(F32)
+    normed = (
+        mixed * lax.rsqrt(jnp.mean(mixed * mixed, axis=-1, keepdims=True) + 1e-05) * norm_gain
+    ).astype(BF16)
     query_width = QH * HD
     keys_vals = jnp.dot(normed, qkv_full[:, query_width:], preferred_element_type=F32).astype(BF16)
-    (kv,) = gather((keys_vals,), (KVH * HD,), seq, 1, "gather_kv")
-    kv = kv.reshape(seq * tokens, 2 * KVH * HD)
+    kv = lax.all_gather(keys_vals, "seq", axis=0, tiled=True)
     queries = jnp.dot(normed, qkv_full[:, :query_width], preferred_element_type=F32).astype(BF16)
     attention = attention_call((queries * HD ** (-0.5)).T, kv)
     return (attention, neuron_energy)

time: 256 us -> 219 us (0.86)
  the two profiles are of different devices: /device:TPU:29 before, /device:TPU:24 now
where the time goes in v3:
time: 219 us; the launch traced here: 218 us
  Pallas kernels  213 us (97%)
  other arithmetic  2.7 us (1%)
    pallas_call x1, Pallas kernels, experts(): pl.pallas_call(functools.partial(experts_kernel, rows, cap), out_shape=[j...  105 us
    pallas_call x1, Pallas kernels, scatter_norm(): pl.pallas_call(functools.partial(scatter_kernel, rows), out_shape=jax.Sha...  65.7 us
    pallas_call x1, Pallas kernels, qkv_attention(): pl.pallas_call(functools.partial(qkv_attention_kernel, rows), out_shape=j...  42.2 us

profile of v3, /device:TPU:24, one launch (start us, length us, event | category | flops | bytes accessed | tf_op | source)
XLA Modules:
  0.0 218.4 jit_solution(7602451356543802612)
XLA Ops:
  0.6 0.7 exponential_reduce_fusion
  1.3 0.7 exponential_divide_fusion
  2.0 0.7 convert_element_type.4
  2.7 0.6 maximum_bitcast_fusion.meta_ref
  3.3 0.7 reshape.18.gain_ref
  4.0 0.0 copy-start
  4.0 104.7 %experts.1 = (bf16[16,128,1536]{2,1,0:T(8,128)(2,1)}, f32[1,768]{1,0:T(1,128)}, bf16[16,96,2560]{2,1,0:T(8,128)(2,1)}) custom-call(bf16[128,1536]{1,0:T(8,128)(2,1)} %x_ref.1, f32[8,128]{1,0:T(8,128)} %maximum_bitcast_fusion.meta_ref, bf16[96,2560]{1,0:T(8,128)(2,1)} %wq_ref.1, bf16[1536,768]{1,0:T(8,128)(2,1)} %bitcast.17, bf16[1536,768]{1,0:T(8,128)(2,1)} %bitcast.18, ...), custom_call_target="tpu_custom_call" | custom-call | tf_op jit(solution)/shard_map/experts/pallas_call | solution.py:298
  108.8 0.0 copy-done
  108.8 65.7 %scatter_norm.1.n_ref = bf16[128,1536]{1,0:T(8,128)(2,1)S(1)} custom-call(bf16[16,128,1536]{2,1,0:T(8,128)(2,1)} %get-tuple-element.5.part_ref, bf16[128,1536]{1,0:T(8,128)(2,1)S(1)} %copy-done, f32[1,1536]{1,0:T(1,128)S(1)} %reshape.18.gain_ref), custom_call_target="tpu_custom_call" | custom-call | bytes 100000000 | tf_op jit(solution)/shard_map/scatter_norm/pallas_call | solution.py:460
  174.5 0.0 copy-start.1
  174.5 0.0 copy-start.2
  174.5 42.2 %qkv_attention.1 = bf16[128,2048]{1,0:T(8,128)(2,1)S(1)} custom-call(bf16[128,1536]{1,0:T(8,128)(2,1)S(1)} %scatter_norm.1.n_ref, bf16[1536,2560]{1,0:T(8,128)(2,1)} %bitcast.16), custom_call_target="tpu_custom_call" | custom-call | tf_op jit(solution)/shard_map/qkv_attention/pallas_call | solution.py:621
  216.7 0.0 copy-done.1
  216.7 0.0 copy-done.2
  216.7 0.3 convolution_bitcast_fusion
  217.0 0.6 copy.14
  217.6 0.8 copy.16
  (1 shorter events, 0.0 us)
Async XLA Ops:
  4.0 104.8 %copy-start = (bf16[128,1536]{1,0:T(8,128)(2,1)S(1)}, bf16[128,1536]{1,0:T(8,128)(2,1)}, u32[]{:S(2)}) copy-start(bf16[128,1536]{1,0:T(8,128)(2,1)} %res_ref.1) | copy-start | bytes 1179652
  174.5 42.2 %copy-start.1 = (f32[1,768]{1,0:T(1,128)S(1)}, f32[1,768]{1,0:T(1,128)}, u32[]{:S(2)}) copy-start(f32[1,768]{1,0:T(1,128)} %get-tuple-element.7) | copy-start | bytes 9220
  174.5 42.2 %copy-start.2 = (s32[1,6]{1,0:T(1,128)S(1)}, s32[1,6]{1,0:T(1,128)}, u32[]{:S(2)}) copy-start(s32[1,6]{1,0:T(1,128)} %param.14) | copy-start | bytes 76

commit v4 on v3

--- a/solution.py
+++ b/solution.py
@@ -240,8 +240,10 @@
     first, second = (2, 0, 1), (3, 4)
     for step in range(rows + 1):
         walk_step(first, step, pass_on, True)
-    walk_step(second, 0, pass_on, True)
+        if step == 2:
+            walk_step(second, 0, pass_on, True)
     from_core(first)
+    walk_step(second, 1, pass_on, True)
     own_copy(0).wait()
     own_copy(1).wait()
 
@@ -284,7 +286,8 @@
             )
             share = jnp.broadcast_to(shares[i], (tokens, tokens)).T[:, :1]
             part_ref[b * batch + i] = (back * share).astype(BF16)
-        walk_step(second, b + 1, pass_on, True)
+        if b + 2 <= rows:
+            walk_step(second, b + 2, pass_on, True)
     from_core(second)
     for step in range(rows + 1):
         walk_step(first + second, step, finish, False)

time: 219 us -> 222 us (1.014)
  the two profiles are of different devices: /device:TPU:24 before, /device:TPU:29 now
where the time goes in v4:
time: 222 us; the launch traced here: 218 us
  Pallas kernels  212 us (95%)
  other arithmetic  2.7 us (1%)
    pallas_call x1, Pallas kernels, experts(): pl.pallas_call(functools.partial(experts_kernel, rows, cap), out_shape=[j...  105 us
    pallas_call x1, Pallas kernels, scatter_norm(): pl.pallas_call(functools.partial(scatter_kernel, rows), out_shape=jax.Sha...  67.4 us
    pallas_call x1, Pallas kernels, qkv_attention(): pl.pallas_call(functools.partial(qkv_attention_kernel, rows), out_shape=j...  40.5 us

profile of v4, /device:TPU:29, one launch (start us, length us, event | category | flops | bytes accessed | tf_op | source)
XLA Modules:
  0.0 218.2 jit_solution(6550557271544005159)
XLA Ops:
  0.6 0.7 exponential_reduce_fusion
  1.3 0.7 exponential_divide_fusion
  2.0 0.7 convert_element_type.4
  2.7 0.6 maximum_bitcast_fusion.meta_ref
  3.3 0.7 reshape.18.gain_ref
  4.0 0.0 copy-start
  4.0 104.5 %experts.1 = (bf16[16,128,1536]{2,1,0:T(8,128)(2,1)}, f32[1,768]{1,0:T(1,128)}, bf16[16,96,2560]{2,1,0:T(8,128)(2,1)}) custom-call(bf16[128,1536]{1,0:T(8,128)(2,1)} %x_ref.1, f32[8,128]{1,0:T(8,128)} %maximum_bitcast_fusion.meta_ref, bf16[96,2560]{1,0:T(8,128)(2,1)} %wq_ref.1, bf16[1536,768]{1,0:T(8,128)(2,1)} %bitcast.17, bf16[1536,768]{1,0:T(8,128)(2,1)} %bitcast.18, ...), custom_call_target="tpu_custom_call" | custom-call | tf_op jit(solution)/shard_map/experts/pallas_call | solution.py:301
  108.5 0.0 copy-done
  108.6 67.4 %scatter_norm.1.n_ref = bf16[128,1536]{1,0:T(8,128)(2,1)S(1)} custom-call(bf16[16,128,1536]{2,1,0:T(8,128)(2,1)} %get-tuple-element.5.part_ref, bf16[128,1536]{1,0:T(8,128)(2,1)S(1)} %copy-done, f32[1,1536]{1,0:T(1,128)S(1)} %reshape.18.gain_ref), custom_call_target="tpu_custom_call" | custom-call | bytes 100000000 | tf_op jit(solution)/shard_map/scatter_norm/pallas_call | solution.py:463
  176.0 0.0 copy-start.1
  176.0 0.0 copy-start.2
  176.0 40.5 %qkv_attention.1 = bf16[128,2048]{1,0:T(8,128)(2,1)S(1)} custom-call(bf16[128,1536]{1,0:T(8,128)(2,1)S(1)} %scatter_norm.1.n_ref, bf16[1536,2560]{1,0:T(8,128)(2,1)} %bitcast.16), custom_call_target="tpu_custom_call" | custom-call | tf_op jit(solution)/shard_map/qkv_attention/pallas_call | solution.py:624
  216.5 0.0 copy-done.1
  216.6 0.0 copy-done.2
  216.6 0.3 convolution_bitcast_fusion
  216.8 0.6 copy.14
  217.5 0.8 copy.16
  (1 shorter events, 0.0 us)
Async XLA Ops:
  4.0 104.5 %copy-start = (bf16[128,1536]{1,0:T(8,128)(2,1)S(1)}, bf16[128,1536]{1,0:T(8,128)(2,1)}, u32[]{:S(2)}) copy-start(bf16[128,1536]{1,0:T(8,128)(2,1)} %res_ref.1) | copy-start | bytes 1179652
  176.0 40.6 %copy-start.1 = (f32[1,768]{1,0:T(1,128)S(1)}, f32[1,768]{1,0:T(1,128)}, u32[]{:S(2)}) copy-start(f32[1,768]{1,0:T(1,128)} %get-tuple-element.7) | copy-start | bytes 9220
  176.0 40.6 %copy-start.2 = (s32[1,6]{1,0:T(1,128)S(1)}, s32[1,6]{1,0:T(1,128)}, u32[]{:S(2)}) copy-start(s32[1,6]{1,0:T(1,128)} %param.14) | copy-start | bytes 76
